TPU v7x, 32 devices: a whole 2x2x4 slice. The times are simulated.
32 devices in a mesh: row: 4 (over z), col: 8 (over y, x, core).
Axes of the slice: x: 2, y: 2, z: 4, core: 2. Of those that a mesh axis runs over, the one named last changes fastest.
Arguments:
- a_blocks: bfloat16 [256, 8, 4, 4096], P('row', 'col'), may hold values from -0.1875 to 0.1875
- a_index: int32 [256, 8, 4], P('row', 'col'), may hold values from 0 to 31, as said below
- p_blocks: bfloat16 [32, 8, 4, 4096], P('row', 'col'), may hold values from -2 to 2
- p_index: int32 [32, 8, 4], P('row', 'col'), may hold values from 0 to 31, as said below
- ap_index: int32 [256, 8], P('row'), may hold values from 0 to 31, as said below
- coarse_index: int32 [32, 8], replicated, may hold values from 0 to 31, as said below
Outputs:
- ap_out: bfloat16 [32, 8, 8, 4096], P('row', 'col')
- coarse_out: float32 [32, 8, 4096], P(('row', 'col'))
Inputs may be any that keep to these rules, and one draw needn't show every extreme that they name: `a_index`: within one (i, c) the 4 entries are distinct. `p_index`: within one row the 4 entries are distinct. `ap_index`: within one row the 8 entries are distinct. `coarse_index`: within one row the 8 entries are distinct.
All inputs are finite; a program needn't handle non-finite values.
Results may differ from a plain program's by a relative error of at most 0.0029.
Values may be sent and summed in bfloat16 or wider, within the bound.
A program may use at most 320 MiB of HBM per device.

v0:
```python
import jax
import jax.numpy as jnp
from jax import lax
from jax.sharding import PartitionSpec as P

B = 64
KA = 4
KP = 4
KAP = 8
KC = 8


def shards(a_blocks, a_index, p_blocks, p_index, ap_index, coarse_index):
    row_count = a_blocks.shape[0]
    own_rows = p_blocks.shape[0]
    col_count = lax.axis_size("col")
    row_axis = lax.axis_size("row")
    gathered_vals, gathered_cols = (
        lax.all_gather(p_blocks, "row", axis=0, tiled=True),
        lax.all_gather(p_index, "row", axis=0, tiled=True),
    )
    group_vals = gathered_vals[:, 0]
    group_cols = gathered_cols[:, 0]
    partial_value = jnp.zeros((row_count, KAP, B, B), jnp.float32)
    for position in range(KA):
        fine_cols = a_index[:, 0, position]
        picked = jnp.take(group_vals, fine_cols, axis=0)
        picked_cols = jnp.take(group_cols, fine_cols, axis=0)
        select = (picked_cols[:, :, None] == ap_index[:, None, :]).astype(jnp.bfloat16)
        chosen = jnp.einsum("rms,rmx->rsx", select, picked, preferred_element_type=jnp.float32)
        chosen = chosen.astype(jnp.bfloat16).reshape(row_count, KAP, B, B)
        jac_block = a_blocks[:, 0, position].reshape(row_count, B, B)
        partial_value = partial_value + jnp.einsum(
            "rax,rsxb->rsab", jac_block, chosen, preferred_element_type=jnp.float32
        )
    summed = lax.psum_scatter(
        partial_value.reshape(own_rows, col_count, KAP, B * B),
        "col",
        scatter_dimension=1,
        tiled=True,
    )
    ap_blocks = summed.astype(jnp.bfloat16)
    own_col = lax.axis_index("col")
    local_slots = lax.dynamic_index_in_dim(
        ap_index.reshape(own_rows, col_count, KAP), own_col, 1, keepdims=False
    )
    prolong_own = p_blocks[:, 0].reshape(own_rows, KP, B, B)
    ap_own = ap_blocks[:, 0].reshape(own_rows, KAP, B, B)
    terms = jnp.einsum("umxa,usxb->umsab", prolong_own, ap_own, preferred_element_type=jnp.float32)
    coarse_rows = p_index[:, 0]
    targets = jnp.take(coarse_index, coarse_rows, axis=0)
    equal = targets[:, :, None, :] == local_slots[:, None, :, None]
    where_slot = jnp.sum(
        jnp.where(equal, lax.broadcasted_iota(jnp.int32, equal.shape, 3), 0), axis=3
    )
    found = jnp.any(equal, axis=3)
    coarse_total = coarse_index.shape[0]
    flat = jnp.where(found, coarse_rows[:, :, None] * KC + where_slot, coarse_total * KC).reshape(
        -1
    )
    coarse_terms = jnp.zeros((coarse_total * KC, B * B), jnp.float32)
    coarse_terms = coarse_terms.at[flat].add(terms.reshape(-1, B * B), mode="drop")
    coarse_terms = coarse_terms.reshape(coarse_total, KC, B * B)
    per_owner = coarse_total // (row_axis * col_count)
    sectioned = coarse_terms.reshape(row_axis, col_count, per_owner, KC, B * B)
    first_sum = lax.psum_scatter(sectioned, "row", scatter_dimension=0, tiled=True)
    second_sum = lax.psum_scatter(first_sum, "col", scatter_dimension=1, tiled=True)
    coarse_out = second_sum.reshape(per_owner, KC, B * B)
    return (ap_blocks, coarse_out)


def solution(mesh):
    placed = (
        P("row", "col", None, None),
        P("row", "col", None),
        P("row", "col", None, None),
        P("row", "col", None),
        P("row", None),
        P(),
    )
    return jax.shard_map(
        shards,
        mesh=mesh,
        in_specs=placed,
        out_specs=(P("row", "col", None, None), P(("row", "col"), None, None)),
        check_vma=False,
    )
```

profile of v0, /device:TPU:0, one launch (start us, length us, event | category | flops | bytes accessed | tf_op | source)
XLA Modules:
  0.0 561.3 jit_solution(12851606825953456484)
XLA Ops:
  7.2 0.7 all-gather.2.cloned.1.call-update
  8.0 2.2 reshape.250
  10.2 0.8 copy.61
  10.9 0.8 reshape.137
  11.7 0.8 copy.58
  12.5 0.7 compare_select_fusion.2
  13.1 0.7 compare_and_fusion.4
  13.8 0.7 bitcast_multiply_fusion
  14.5 0.8 compare_and_fusion
  15.4 14.9 %all_gather.6 = s32[32,1,4]{2,1,0:T(1,128)S(1)} all-gather(s32[8,1,4]{2,1,0:T(1,128)S(1)} %copy.58), channel_id=1, replica_groups=mesh['row'=4,'col'=8] {'row'}, dimensions={0}, use_global_device_ids=true | all-gather | bytes 640 | tf_op jit(solution)/shard_map/all_gather | solution.py:20
  30.3 0.1 copy.59
  30.4 0.1 copy.60
  30.5 0.6 gather_fusion.3
  31.1 0.6 gather_fusion.1
  31.7 14.5 %slice_reduce_fusion = (bf16[64,4096]{1,0:T(8,128)(2,1)S(1)}, bf16[64,4096]{1,0:T(8,128)(2,1)S(1)}, bf16[64,4096]{1,0:T(8,128)(2,1)S(1)}, bf16[64,4096]{1,0:T(8,128)(2,1)S(1)}) fusion(bf16[64,1,4,4096]{3,2,1,0:T(4,128)(2,1)} %param.10), kind=kLoop, calls=%fused_computation.39 | loop fusion | bytes 4194304 | tf_op jit(solution)/shard_map/slice | solution.py:32
  46.2 2.1 reshape.246
  48.4 1.1 reshape.245
  49.5 0.6 gather_fusion.5
  50.1 0.6 gather_fusion.7
  50.7 2.1 reshape.247
  52.8 1.1 reshape.248
  54.0 0.1 constant_dynamic-slice_fusion
  54.0 0.1 copy.73
  54.2 0.1 copy.72
  54.2 0.1 copy.71
  54.3 0.1 reshape.206
  54.4 0.1 copy.70
  54.5 0.1 copy.74
  54.6 0.6 gather_fusion
  55.2 0.1 broadcast_select_fusion.4
  55.2 0.7 compare_reduce_fusion
  55.9 0.7 fusion.23
  56.7 0.1 add_select_fusion
  56.7 0.1 select_n.76
  56.9 0.6 dynamic-slice
  57.4 0.1 broadcast_select_fusion.2
  57.5 0.1 broadcast_select_fusion
  57.7 4.9 gather_fusion.4
  62.6 3.6 gather_fusion.2
  66.1 3.5 gather_fusion.6
  69.7 3.6 gather_fusion.8
  73.4 4.5 convolution_convert_fusion.2
  77.9 12.6 %reshape.133 = bf16[64,8,64,64]{3,2,1,0:T(8,128)(2,1)} reshape(bf16[64,8,4096]{2,1,0:T(8,128)(2,1)} %convolution_convert_fusion.2) | data formatting | bytes 8388608 | tf_op jit(solution)/shard_map/reshape | solution.py:31
  90.5 4.5 convolution_convert_fusion.3
  95.0 12.6 %reshape.132 = bf16[64,8,64,64]{3,2,1,0:T(8,128)(2,1)} reshape(bf16[64,8,4096]{2,1,0:T(8,128)(2,1)} %convolution_convert_fusion.3) | data formatting | bytes 8388608 | tf_op jit(solution)/shard_map/reshape | solution.py:31
  107.5 4.5 convolution_convert_fusion.1
  112.0 12.6 %reshape.134 = bf16[64,8,64,64]{3,2,1,0:T(8,128)(2,1)} reshape(bf16[64,8,4096]{2,1,0:T(8,128)(2,1)} %convolution_convert_fusion.1) | data formatting | bytes 8388608 | tf_op jit(solution)/shard_map/reshape | solution.py:31
  124.6 4.5 convolution_convert_fusion
  129.1 12.8 %reshape.135 = bf16[64,8,64,64]{3,2,1,0:T(8,128)(2,1)} reshape(bf16[64,8,4096]{2,1,0:T(8,128)(2,1)} %convolution_convert_fusion) | data formatting | bytes 8388608 | tf_op jit(solution)/shard_map/reshape | solution.py:31
  141.9 11.5 %fusion.14 = f32[64,8,64,64]{3,2,1,0:T(8,128)} fusion(bf16[64,8,64,64]{3,2,1,0:T(8,128)(2,1)} %reshape.133, bf16[64,64,64,1]{2,1,0,3:T(8,128)(2,1)S(1)} %copy-done.1), kind=kOutput, calls=%fused_computation.31 | convolution fusion | flops 268435456 | bytes 13107200 | tf_op jit(solution)/shard_map/rax,rsxb->rsab/dot_general | solution.py:33
  153.4 11.6 %fusion.16 = f32[64,8,64,64]{3,2,1,0:T(8,128)} fusion(bf16[64,8,64,64]{3,2,1,0:T(8,128)(2,1)} %reshape.132, bf16[64,64,64,1]{2,1,0,3:T(8,128)(2,1)S(1)} %reshape.245), kind=kOutput, calls=%fused_computation.33 | convolution fusion | flops 268435456 | bytes 13107200 | tf_op jit(solution)/shard_map/rax,rsxb->rsab/dot_general | solution.py:33
  165.0 11.5 %fusion.12 = f32[64,8,64,64]{3,2,1,0:T(8,128)} fusion(bf16[64,8,64,64]{3,2,1,0:T(8,128)(2,1)} %reshape.134, bf16[64,64,64,1]{2,1,0,3:T(8,128)(2,1)S(1)} %copy-done.2), kind=kOutput, calls=%fused_computation.29 | convolution fusion | flops 268435456 | bytes 13107200 | tf_op jit(solution)/shard_map/rax,rsxb->rsab/dot_general | solution.py:33
  176.5 25.5 %add_bitcast_fusion = f32[64,8,64,64]{2,3,1,0:T(8,128)} fusion(f32[64,8,64,64]{3,2,1,0:T(8,128)} %fusion.12, f32[64,8,64,64]{3,2,1,0:T(8,128)} %fusion.16, f32[64,8,64,64]{3,2,1,0:T(8,128)} %fusion.14, bf16[64,8,64,64]{3,2,1,0:T(8,128)(2,1)} %reshape.135, bf16[64,64,64,1]{2,1,0,3:T(8,128)(2,1)S(1)} %reshape.248), kind=kOutput, calls=%fused_computation.10 | convolution fusion | flops 274726912 | bytes 38273024 | tf_op jit(solution)/shard_map/rax,rsxb->rsab/dot_general | solution.py:33
  202.0 17.5 %copy.69 = f32[64,8,64,64]{3,2,1,0:T(8,128)} copy(f32[64,8,64,64]{2,3,1,0:T(8,128)} %add_bitcast_fusion) | data formatting | bytes 16777216 | tf_op jit(solution)/shard_map/add | solution.py:33
  219.4 14.8 %reshape.136 = f32[8,8,8,4096]{3,2,1,0:T(8,128)} reshape(f32[64,8,64,64]{3,2,1,0:T(8,128)} %copy.69) | data formatting | bytes 16777216 | tf_op jit(solution)/shard_map/reshape | solution.py:37
  234.2 166.4 %all-reduce.2 = bf16[8,8,8,4096]{3,2,1,0:T(8,128)(2,1)} all-reduce(f32[8,8,8,4096]{3,2,1,0:T(8,128)} %reshape.136), channel_id=2, replica_groups=mesh['row'=4,'col'=8] {'col'}, use_global_device_ids=true, to_apply=%region_0.3.clone | all-reduce | flops 2097152 | bytes 12582912
  400.6 1.7 dynamic-slice_convert_fusion
  402.3 1.1 reshape_squeeze.22
  403.5 4.5 convolution_bitcast_fusion
  408.0 9.1 %copy.76 = f32[8,4,8,64,64]{4,3,2,1,0:T(8,128)} copy(f32[8,4,8,64,64]{3,4,1,2,0:T(8,128)} %convolution_bitcast_fusion) | data formatting | bytes 8388608 | tf_op jit(solution)/shard_map/umxa,usxb->umsab/transpose | solution.py:49
  417.1 7.9 %reshape.216 = f32[256,4096]{1,0:T(8,128)} reshape(f32[8,4,8,64,64]{4,3,2,1,0:T(8,128)} %copy.76) | data formatting | bytes 8388608 | tf_op jit(solution)/shard_map/reshape | solution.py:62
  425.0 9.6 %scatter_custom_fusion = f32[256,4096]{1,0:T(8,128)} fusion(s32[256]{0:T(256)S(1)} %bitcast.76, f32[256,4096]{1,0:T(8,128)} %reshape.216, f32[]{:T(128)} %constant.25.clone.1), kind=kCustom, calls=%fused_computation.20 | custom fusion | flops 1048576 | bytes 4194816 | tf_op jit(solution)/shard_map/scatter-add | solution.py:62
  434.7 79.1 %reduce-scatter.4.cloned.1.call-done = f32[1,8,1,8,4096]{4,3,2,1,0:T(8,128)} async-done(((f32[4,8,1,8,4096]{4,3,2,1,0:T(8,128)}), f32[1,8,1,8,4096]{4,3,2,1,0:T(8,128)}) %reduce-scatter.4.cloned.1.call-update) | async-done | bytes 1048592 | tf_op jit(solution)/shard_map/reduce_scatter | solution.py:66
  513.8 40.6 %reduce-scatter.6.cloned.1.call-done = f32[1,1,1,8,4096]{4,3,2,1,0:T(8,128)} async-done(((f32[1,8,1,8,4096]{4,3,2,1,0:T(8,128)}), f32[1,1,1,8,4096]{4,3,2,1,0:T(8,128)}) %reduce-scatter.6.cloned.1.call-update) | async-done | bytes 131088 | tf_op jit(solution)/shard_map/reduce_scatter | solution.py:67
  (26 shorter events, 0.2 us)
Async XLA Ops:
  7.2 50.5 %all-gather.2.cloned.1.call-start = ((), (), s32[]{:S(2)}) async-start(), calls=%async_computation.2 | async-start | bytes 1310720 | tf_op jit(solution)/shard_map/all_gather | solution.py:19
  7.9 505.9 %reduce-scatter.4.cloned.1.call-start = ((), (), s32[]{:S(2)}) async-start(), calls=%async_computation.3 | async-start | bytes 5242880 | tf_op jit(solution)/shard_map/reduce_scatter | solution.py:66
  46.2 8.0 %copy-start.5 = (s32[32,8]{0,1:T(8,128)S(1)}, s32[32,8]{0,1:T(8,128)}, u32[]{:S(2)}) copy-start(s32[32,8]{0,1:T(8,128)} %param.15) | copy-start | bytes 3076
  46.2 10.6 %copy-start.6 = (u32[32]{0:T(128)S(1)}, u32[32]{0:T(128)}, u32[]{:S(2)}) copy-start(u32[32]{0:T(128)} %constant.61) | copy-start | bytes 388
  57.7 4.9 copy-start
  129.1 12.8 %copy-start.1 = (bf16[64,64,64,1]{2,1,0,3:T(8,128)(2,1)S(1)}, bf16[64,64,64,1]{2,1,0,3:T(8,128)(2,1)}, u32[]{:S(2)}) copy-start(bf16[64,64,64,1]{2,1,0,3:T(8,128)(2,1)} %reshape.246) | copy-start | bytes 1572868
  153.4 11.6 %copy-start.2 = (bf16[64,64,64,1]{2,1,0,3:T(8,128)(2,1)S(1)}, bf16[64,64,64,1]{2,1,0,3:T(8,128)(2,1)}, u32[]{:S(2)}) copy-start(bf16[64,64,64,1]{2,1,0,3:T(8,128)(2,1)} %reshape.247) | copy-start | bytes 1572868
  234.2 169.3 %copy-start.3 = (bf16[8,4,64,64,1]{3,2,1,0,4:T(8,128)(2,1)S(1)}, bf16[8,4,64,64,1]{3,2,1,0,4:T(8,128)(2,1)}, u32[]{:S(2)}) copy-start(bf16[8,4,64,64,1]{3,2,1,0,4:T(8,128)(2,1)} %reshape.250) | copy-start | bytes 786436
  402.3 5.7 %copy-start.4 = (bf16[8,1,8,4096]{3,2,1,0:T(8,128)(2,1)}, bf16[8,1,8,4096]{3,2,1,0:T(8,128)(2,1)S(1)}, u32[]{:S(2)}) copy-start(bf16[8,1,8,4096]{3,2,1,0:T(8,128)(2,1)S(1)} %dynamic-slice_convert_fusion) | copy-start | bytes 1572868
  434.7 119.8 %reduce-scatter.6.cloned.1.call-start = ((), (), s32[]{:S(2)}) async-start(), calls=%async_computation.4 | async-start | bytes 1179648 | tf_op jit(solution)/shard_map/reduce_scatter | solution.py:67
Sparse Core Ops, SparseCore 0:
  9.6 30.7 all-gather.1
  434.8 78.9 reduce-scatter.3
  517.9 36.5 reduce-scatter.5
where the time goes:
time: 568 us; the launch traced here: 561 us
  blocking collectives  181 us (32%)
  local copies, waits for them, and re-layouts  148 us (26%)
  waiting for transfers between devices  120 us (21%)
  matrix products  82.5 us (15%)
  between operations  14.4 us (3%)
  other arithmetic  14.3 us (3%)
    unnamed x1, blocking collectives  166 us
    reduce_scatter x1, waiting for transfers between devices, shards(): lax.psum_scatter(sectioned, 'row', scatter_dimension=0, tiled=True)  79.1 us
    dot_general x4, matrix products, shards(): jnp.einsum('rax,rsxb->rsab', jac_block, chosen, preferred_element_type=jn...  60 us
    reshape x4, local copies, waits for them, and re-layouts, shards(): chosen = chosen.astype(jnp.bfloat16).reshape(row_count, KAP, B, B)  50.5 us
    reduce_scatter x1, waiting for transfers between devices, shards(): lax.psum_scatter(first_sum, 'col', scatter_dimension=1, tiled=True)  40.6 us
    dot_general x4, matrix products, shards(): jnp.einsum('rms,rmx->rsx', select, picked, preferred_element_type=jnp.flo...  18 us
    add x1, local copies, waits for them, and re-layouts, shards(): partial_value + jnp.einsum('rax,rsxb->rsab', jac_block, chosen, preferred...  17.5 us
    gather x4, local copies, waits for them, and re-layouts, shards(): picked = jnp.take(group_vals, fine_cols, axis=0)  15.6 us
  transfers between devices with their start and end apart: 3, of which 2 were waited for; matrix products, arithmetic and copies ran while one was open for 6% of the time, Pallas kernels for 0%

commit v1 on v0

v1 whole, which is shorter than its diff:
```python
import functools

import jax
import jax.numpy as jnp
from jax import lax
from jax.experimental import pallas as pl
from jax.experimental.pallas import tpu as pltpu
from jax.sharding import PartitionSpec as P

MESH = pl.DeviceIdType.MESH
F32 = jnp.float32
BF16 = jnp.bfloat16


def left_mask(half):
    return lax.broadcasted_iota(jnp.int32, (half, 4 * half), 1) < 2 * half


def swap(x):
    return pltpu.roll(x, x.shape[1] // 2, 1)


def halves(x, left):
    other = swap(x)
    zero = jnp.zeros_like(x)
    in_left = jnp.concatenate([jnp.where(left, x, zero), jnp.where(left, other, zero)], axis=0)
    in_right = jnp.concatenate([jnp.where(left, zero, other), jnp.where(left, zero, x)], axis=0)
    return in_left.astype(BF16), in_right.astype(BF16)


def interleave(tile, left):
    half = left.shape[0]
    top, bottom = tile[:half], tile[half:]
    return jnp.where(left, top, swap(bottom)), jnp.where(left, swap(top), bottom)


def gather_tiles(in_left, in_right, picks):
    return jnp.concatenate(
        [in_left[picks[n]] + in_right[picks[n + 1]] for n in range(0, len(picks), 2)], axis=1
    )


def kernel(
    sizes, a_ref, pg_ref, pown_ref, order_ref, aidx_ref, pidx_ref, sidx_ref,
    ap_out, coarse_out,
    pl_l, pl_r, pt_l, pt_r, apl, apr,
    s1a, r1a, s2a, r2a, acc_a, s1b, r1b, s2b, r2b, acc_b, r3,
    s1a_send, s1a_recv, s2a_send, s2a_recv, s1b_send, s1b_recv, s2b_send, s2b_recv, s3_send, s3_recv,
):
    rows, cols, own, ka, kp, kap, kc, per, groups = sizes
    chips = cols // 2
    half = pg_ref.shape[1]
    width = 2 * half
    left = left_mask(half)
    row, col = lax.axis_index("row"), lax.axis_index("col")
    core = lax.rem(col, 2)
    chip = col // 2
    partner = chip * 2 + 1 - core

    barrier = pltpu.get_barrier_semaphore()
    pl.semaphore_signal(barrier, inc=1, device_id=(row, partner), device_id_type=MESH)
    for d in range(1, chips):
        there = lax.rem(chip + d, chips) * 2 + core
        pl.semaphore_signal(barrier, inc=1, device_id=(row, there), device_id_type=MESH)
    for d in range(1, rows):
        pl.semaphore_signal(
            barrier, inc=1, device_id=(lax.rem(row + d, rows), col), device_id_type=MESH
        )

    def spread(n, carry):
        in_left, in_right = halves(pg_ref[n].astype(F32), left)
        pl_l[n] = in_left
        pl_r[n] = in_right
        return carry

    lax.fori_loop(0, groups, spread, 0, unroll=4)
    pl_l[groups] = jnp.zeros(pl_l.shape[1:], BF16)
    pl_r[groups] = jnp.zeros(pl_r.shape[1:], BF16)
    pl.semaphore_wait(barrier, chips + rows - 1)

    def product_row(to, u):
        i = u * cols + to
        lhs = []
        for e in range(0, ka, 2):
            x0, x1 = a_ref[i, e].astype(F32), a_ref[i, e + 1].astype(F32)
            top = jnp.where(left, x0, swap(x1))
            bottom = jnp.where(left, swap(x0), x1)
            lhs.append(jnp.concatenate([top, bottom], axis=0).astype(BF16))
        base = i * (ka * kap)
        rhs = [
            gather_tiles(pl_l, pl_r, [aidx_ref[base + e * kap + s] for s in range(kap)])
            for e in range(ka)
        ]
        return jnp.dot(
            jnp.concatenate(lhs, axis=1), jnp.concatenate(rhs, axis=0), preferred_element_type=F32
        )

    def coarse_row(to, n):
        j = ((n // per) * cols + to) * per + lax.rem(n, per)
        lhs = gather_tiles(pt_l, pt_r, [pidx_ref[j * own + u] for u in range(own)])
        rhs = [
            gather_tiles(apl, apr, [sidx_ref[(j * own + u) * kc + t] for t in range(kc)])
            for u in range(own)
        ]
        return jnp.dot(lhs, jnp.concatenate(rhs, axis=0), preferred_element_type=F32)

    def reduce_plane(compute, count, s1, r1, s2, r2, acc, sems, before_wait):
        s1_send, s1_recv, s2_send, s2_recv = sems
        order = list(range(1, chips)) + [0]
        first, second = [], []

        def give(n):
            d = order[n]
            to = lax.rem(chip + d, chips) * 2 + 1 - core
            slot = n % s1.shape[0]
            if n >= s1.shape[0]:
                first[n - s1.shape[0]].wait_send()

            def body(k, carry):
                s1[slot, k] = compute(to, k)
                return carry

            lax.fori_loop(0, count, body, 0)
            copy = pltpu.make_async_remote_copy(
                src_ref=s1.at[slot], dst_ref=r1.at[n], send_sem=s1_send.at[n], recv_sem=s1_recv.at[n],
                device_id=(row, partner), device_id_type=MESH,
            )
            copy.start()
            first.append(copy)

        def finish(n):
            d = order[n]
            to = lax.rem(chip + d, chips) * 2 + core
            slot = n % s2.shape[0]
            first[n].wait_recv()
            if d and n >= s2.shape[0]:
                second[n - s2.shape[0]].wait_send()

            def body(k, carry):
                value = compute(to, k) + r1[n, k]
                if d:
                    s2[slot, k] = value.astype(s2.dtype)
                else:
                    acc[k] = value
                return carry

            lax.fori_loop(0, count, body, 0)
            if d:
                copy = pltpu.make_async_remote_copy(
                    src_ref=s2.at[slot], dst_ref=r2.at[n], send_sem=s2_send.at[n], recv_sem=s2_recv.at[n],
                    device_id=(row, to), device_id_type=MESH,
                )
                copy.start()
                second.append(copy)

        for n in range(chips):
            give(n)
            if n:
                finish(n - 1)
        finish(chips - 1)
        before_wait()
        for n in range(max(0, chips - s1.shape[0]), chips):
            first[n].wait_send()
        for copy in second:
            copy.wait_recv()
        for n in range(max(0, chips - 1 - s2.shape[0]), chips - 1):
            second[n].wait_send()

        def total(k):
            value = acc[k]
            for n in range(chips - 1):
                value = value + r2[n, k].astype(F32)
            return value

        return total

    def turn_prolongator():
        order_mat = order_ref[...]

        def body(n, carry):
            block = halves(pown_ref[n].astype(F32), left)[0]
            zero = jnp.zeros_like(block)
            contract = (((1,), (1,)), ((), ()))
            pt_l[n] = lax.dot_general(
                order_mat, jnp.concatenate([block, zero], axis=0), contract, preferred_element_type=F32
            ).astype(BF16)
            pt_r[n] = lax.dot_general(
                order_mat, jnp.concatenate([zero, block], axis=0), contract, preferred_element_type=F32
            ).astype(BF16)
            return carry

        lax.fori_loop(0, own * kp, body, 0, unroll=2)
        pt_l[own * kp] = jnp.zeros(pt_l.shape[1:], BF16)
        pt_r[own * kp] = jnp.zeros(pt_r.shape[1:], BF16)

    total = reduce_plane(
        product_row, own, s1a, r1a, s2a, r2a, acc_a, (s1a_send, s1a_recv, s2a_send, s2a_recv), turn_prolongator
    )

    def keep(u, carry):
        value = total(u).astype(BF16).astype(F32)
        for s in range(0, kap, 2):
            tile = value[:, s * width : (s + 2) * width]
            x0, x1 = interleave(tile, left)
            ap_out[u, s] = x0.astype(BF16)
            ap_out[u, s + 1] = x1.astype(BF16)
            for n, x in ((s, x0), (s + 1, x1)):
                in_left, in_right = halves(x, left)
                apl[u * kap + n] = in_left
                apr[u * kap + n] = in_right
        return carry

    lax.fori_loop(0, own, keep, 0)
    apl[own * kap] = jnp.zeros(apl.shape[1:], BF16)
    apr[own * kap] = jnp.zeros(apr.shape[1:], BF16)

    coarse_total = reduce_plane(
        coarse_row, rows * per, s1b, r1b, s2b, r2b, acc_b, (s1b_send, s1b_recv, s2b_send, s2b_recv), lambda: None
    )

    def gather_sum(n, carry):
        acc_b[n] = coarse_total(n)
        return carry

    lax.fori_loop(0, rows * per, gather_sum, 0)
    third = []
    for d in range(1, rows):
        to = lax.rem(row + d, rows)
        copy = pltpu.make_async_remote_copy(
            src_ref=acc_b.at[pl.ds(to * per, per)], dst_ref=r3.at[d - 1],
            send_sem=s3_send.at[d - 1], recv_sem=s3_recv.at[d - 1],
            device_id=(to, col), device_id_type=MESH,
        )
        copy.start()
        third.append(copy)
    for copy in third:
        copy.wait()
    for q in range(per):
        value = acc_b[row * per + q]
        for d in range(1, rows):
            value = value + r3[d - 1, q]
        for t in range(0, kc, 2):
            x0, x1 = interleave(value[:, t * width : (t + 2) * width], left)
            coarse_out[q, t] = x0
            coarse_out[q, t + 1] = x1


def shards(a_blocks, a_index, p_blocks, p_index, ap_index, coarse_index):
    rows, cols = lax.axis_size("row"), lax.axis_size("col")
    count, _, ka, flat = a_blocks.shape
    own, _, kp, _ = p_blocks.shape
    kap = ap_index.shape[1]
    coarse, kc = coarse_index.shape
    per = coarse // (rows * cols)
    width = int(round(flat ** 0.5))
    half = width // 2
    lanes = 2 * width

    a2 = a_blocks.reshape(count, ka, half, lanes)
    p2 = p_blocks.reshape(own * kp, half, lanes)
    p_nat = p_blocks.reshape(own * kp, 2, half, width).transpose(0, 2, 1, 3).reshape(own * kp, half, lanes)
    group = lax.all_gather(p_nat, "row", axis=0, tiled=True)
    group_cols = lax.all_gather(p_index[:, 0], "row", axis=0, tiled=True)
    groups = group.shape[0]

    fine = a_index[:, 0]
    hot = fine[:, :, None, None] == lax.broadcasted_iota(jnp.int32, (1, 1, group_cols.shape[0], 1), 2)
    picked = jnp.sum(jnp.where(hot, group_cols[None, None], 0), axis=2)
    same = picked[:, :, :, None] == ap_index[:, None, None, :]
    place = fine[:, :, None, None] * kp + lax.broadcasted_iota(jnp.int32, (1, 1, kp, 1), 2)
    a_pick = jnp.where(jnp.any(same, axis=2), jnp.sum(jnp.where(same, place, 0), axis=2), groups)

    mine = p_index[:, 0]
    slots = lax.dynamic_index_in_dim(ap_index.reshape(own, cols, kap), lax.axis_index("col"), 1, keepdims=False)
    which = jnp.arange(own * kp, dtype=jnp.int32).reshape(own, kp)
    hit = mine[None] == jnp.arange(coarse, dtype=jnp.int32)[:, None, None]
    p_pick = jnp.where(jnp.any(hit, axis=2), jnp.sum(jnp.where(hit, which[None], 0), axis=2), own * kp)
    spot = jnp.arange(own * kap, dtype=jnp.int32).reshape(own, kap)
    match = coarse_index[:, None, :, None] == slots[None, :, None, :]
    s_pick = jnp.where(
        jnp.any(match, axis=3), jnp.sum(jnp.where(match, spot[None, :, None, :], 0), axis=3), own * kap
    )

    into = jnp.arange(width, dtype=jnp.int32)
    source = (into % half) * 2 + into // half
    order_mat = (source[:, None] == jnp.arange(lanes, dtype=jnp.int32)[None, :]).astype(BF16)

    chips = cols // 2
    others = max(chips - 1, 1)
    slots2 = min(others, 3)
    wide = kap * width
    wide_c = kc * width
    vmem = pl.BlockSpec(memory_space=pltpu.VMEM)
    smem = pl.BlockSpec(memory_space=pltpu.SMEM)
    dma = pltpu.SemaphoreType.DMA
    n_coarse = rows * per
    ap, coarse_out = pl.pallas_call(
        functools.partial(kernel, (rows, cols, own, ka, kp, kap, kc, per, groups)),
        out_shape=(
            jax.ShapeDtypeStruct((own, kap, half, lanes), BF16),
            jax.ShapeDtypeStruct((per, kc, half, lanes), F32),
        ),
        in_specs=[vmem, vmem, vmem, vmem, smem, smem, smem],
        out_specs=(vmem, vmem),
        scratch_shapes=[
            pltpu.VMEM((groups + 1, width, lanes), BF16),
            pltpu.VMEM((groups + 1, width, lanes), BF16),
            pltpu.VMEM((own * kp + 1, width, lanes), BF16),
            pltpu.VMEM((own * kp + 1, width, lanes), BF16),
            pltpu.VMEM((own * kap + 1, width, lanes), BF16),
            pltpu.VMEM((own * kap + 1, width, lanes), BF16),
            pltpu.VMEM((2, own, width, wide), F32),
            pltpu.VMEM((chips, own, width, wide), F32),
            pltpu.VMEM((slots2, own, width, wide), BF16),
            pltpu.VMEM((others, own, width, wide), BF16),
            pltpu.VMEM((own, width, wide), F32),
            pltpu.VMEM((2, n_coarse, width, wide_c), F32),
            pltpu.VMEM((chips, n_coarse, width, wide_c), F32),
            pltpu.VMEM((slots2, n_coarse, width, wide_c), F32),
            pltpu.VMEM((others, n_coarse, width, wide_c), F32),
            pltpu.VMEM((n_coarse, width, wide_c), F32),
            pltpu.VMEM((max(rows - 1, 1), per, width, wide_c), F32),
            dma((chips,)), dma((chips,)), dma((others,)), dma((others,)),
            dma((chips,)), dma((chips,)), dma((others,)), dma((others,)),
            dma((max(rows - 1, 1),)), dma((max(rows - 1, 1),)),
        ],
        compiler_params=pltpu.CompilerParams(
            collective_id=0, has_side_effects=True, vmem_limit_bytes=60 * 1024 * 1024
        ),
    )(a2, group, p2, order_mat, a_pick.reshape(-1), p_pick.reshape(-1), s_pick.reshape(-1))
    return ap.reshape(own, 1, kap, flat), coarse_out.reshape(per, kc, flat)


def solution(mesh):
    placed = (
        P("row", "col", None, None),
        P("row", "col", None),
        P("row", "col", None, None),
        P("row", "col", None),
        P("row", None),
        P(),
    )
    return jax.shard_map(
        shards,
        mesh=mesh,
        in_specs=placed,
        out_specs=(P("row", "col", None, None), P(("row", "col"), None, None)),
        check_vma=False,
    )
```

time: 568 us -> 135 us (0.24)
  blocking collectives: 181 us -> 14.9 us
  local copies, waits for them, and re-layouts: 148 us -> 13.8 us
  waiting for transfers between devices: 120 us -> 7.35 us
  matrix products: 82.5 us -> 0 us
  Pallas kernels: 0 us -> 81.7 us
  other arithmetic: 14.3 us -> 1.37 us
    unnamed x1 -> x0, blocking collectives: 166 us -> none
    reduce_scatter x2 -> x0, waiting for transfers between devices: 120 us -> none  [the longest x1 79.1 us: shards(): lax.psum_scatter(sectioned, 'row', scatter_dimension=0, tiled=True)]
    dot_general x9 -> x0, matrix products: 82.5 us -> none  [the longest x4 60 us: shards(): jnp.einsum('rax,rsxb->rsab', jac_block, chosen, preferred_element_type=jn...]
    pallas_call x0 -> x1, Pallas kernels: none -> 81.7 us  [shards(): pl.pallas_call(functools.partial(kernel, (rows, cols, own, ka, kp, kap, k...]
    reshape x7 -> x8, local copies, waits for them, and re-layouts: 73.9 us -> 11 us  [the longest x2 3.65 us: shards(): return (ap.reshape(own, 1, kap, flat), coarse_out.reshape(per, kc, flat))]
    gather x9 -> x0, local copies, waits for them, and re-layouts: 18.5 us -> none  [the longest x4 15.6 us: shards(): picked = jnp.take(group_vals, fine_cols, axis=0)]
    add x1 -> x0, local copies, waits for them, and re-layouts: 17.5 us -> none  [shards(): partial_value + jnp.einsum('rax,rsxb->rsab', jac_block, chosen, preferred...]
    slice x1 -> x0, local copies, waits for them, and re-layouts: 14.5 us -> none  [shards(): jac_block = a_blocks[:, 0, position].reshape(row_count, B, B)]
  transfers between devices with their start and end apart: 3 -> 1, of which waited for: 2 -> 1; matrix products, arithmetic and copies ran while one was open for 6% -> 6% of each run, Pallas kernels for 0% -> 0%
where the time goes in v1:
time: 135 us; the launch traced here: 133 us
  Pallas kernels  81.7 us (61%)
  blocking collectives  14.9 us (11%)
  between operations  14.2 us (11%)
  local copies, waits for them, and re-layouts  13.8 us (10%)
  waiting for transfers between devices  7.35 us (5%)
  other arithmetic  1.37 us (1%)
    pallas_call x1, Pallas kernels, shards(): pl.pallas_call(functools.partial(kernel, (rows, cols, own, ka, kp, kap, k...  81.7 us
    all_gather x1, blocking collectives, shards(): group_cols = lax.all_gather(p_index[:, 0], 'row', axis=0, tiled=True)  14.9 us
    all_gather x1, waiting for transfers between devices, shards(): group = lax.all_gather(p_nat, 'row', axis=0, tiled=True)  7.33 us
    reshape x2, local copies, waits for them, and re-layouts, shards(): return (ap.reshape(own, 1, kap, flat), coarse_out.reshape(per, kc, flat))  3.65 us
    reshape x1, local copies, waits for them, and re-layouts, shards(): a2 = a_blocks.reshape(count, ka, half, lanes)  3.25 us
    reshape x3, local copies, waits for them, and re-layouts, shards(): p_blocks.reshape(own * kp, 2, half, width).transpose(0, 2, 1, 3)  3.03 us
  transfers between devices with their start and end apart: 1, of which 1 were waited for; matrix products, arithmetic and copies ran while one was open for 6% of the time, Pallas kernels for 0%

profile of v1, /device:TPU:0, one launch (start us, length us, event | category | flops | bytes accessed | tf_op | source)
XLA Modules:
  0.0 133.3 jit_solution(2139338492554704703)
XLA Ops:
  7.2 0.0 copy-start.1
  7.2 0.0 copy-start.3
  7.2 0.0 copy-start.2
  7.2 0.0 copy-start.4
  7.2 0.0 copy-start.5
  7.2 0.0 copy-start
  7.2 0.0 all-gather.3.cloned.1.call-start
  7.3 1.6 %reshape.115 = bf16[32,2,32,64]{3,2,1,0:T(8,128)(2,1)S(1)} reshape(bf16[8,1,4,4096]{3,2,1,0:T(4,128)(2,1)} %param.8) | data formatting | bytes 524288 | tf_op jit(solution)/shard_map/reshape | solution.py:261
  8.8 0.5 copy.45
  9.4 1.0 reshape.116
  10.3 0.0 all-gather.3.cloned.1.call-update
  10.4 0.0 copy-done.1
  10.4 1.0 reshape.117.pown_ref
  11.4 0.0 copy-done.3
  11.4 0.1 copy.37
  11.4 0.1 fusion.3
  11.5 0.1 select_reduce_fusion.1
  11.6 14.9 %all-gather = s32[32,1,4]{2,1,0:T(1,128)S(1)} all-gather(s32[8,1,4]{2,1,0:T(1,128)S(1)} %copy.37), channel_id=2, replica_groups=mesh['row'=4,'col'=8] {'row'}, dimensions={0}, use_global_device_ids=true | all-gather | bytes 640 | tf_op jit(solution)/shard_map/all_gather | solution.py:263
  26.5 0.1 copy.38
  26.6 0.1 copy.40
  26.6 0.7 select_n.72.pidx_ref
  27.3 0.0 copy-done.2
  27.3 0.1 reshape.118
  27.4 0.1 constant_dynamic-slice_fusion
  27.5 0.1 copy.41
  27.6 0.0 copy-done.4
  27.6 0.2 compare_reduce_fusion
  27.8 0.2 fusion
  28.0 0.1 copy.42
  28.1 0.7 select_n.76.sidx_ref
  28.8 0.0 copy-done.5
  28.8 0.1 select_reduce_fusion
  29.0 0.1 copy.39
  29.1 0.8 select_n.69.aidx_ref
  29.9 0.0 copy-done
  29.9 3.3 %reshape.114.a_ref = bf16[64,4,32,128]{3,2,1,0:T(8,128)(2,1)} reshape(bf16[64,1,4,4096]{3,2,1,0:T(4,128)(2,1)S(1)} %copy-done) | data formatting | bytes 4194304 | tf_op jit(solution)/shard_map/reshape | solution.py:259
  33.2 0.7 fusion.2.order_ref
  33.8 7.3 %all-gather.3.cloned.1.call-done.pg_ref = bf16[128,32,128]{2,1,0:T(8,128)(2,1)} async-done(((bf16[32,32,128]{2,1,0:T(8,128)(2,1)}), bf16[128,32,128]{2,1,0:T(8,128)(2,1)}) %all-gather.3.cloned.1.call-update) | async-done | bytes 1048592 | tf_op jit(solution)/shard_map/all_gather | solution.py:262
  41.2 81.7 %shard_map.77 = (bf16[8,8,32,128]{3,2,1,0:T(8,128)(2,1)}, f32[1,8,32,128]{3,2,1,0:T(8,128)}) custom-call(bf16[64,4,32,128]{3,2,1,0:T(8,128)(2,1)} %reshape.114.a_ref, bf16[128,32,128]{2,1,0:T(8,128)(2,1)} %all-gather.3.cloned.1.call-done.pg_ref, bf16[32,32,128]{2,1,0:T(8,128)(2,1)} %reshape.117.pown_ref, bf16[64,128]{1,0:T(8,128)(2,1)} %fusion.2.order_ref, ...), custom_call_target="tpu_custom_call" | custom-call | tf_op jit(solution)/shard_map/pallas_call | solution.py:297
  122.9 2.1 %reshape.119 = bf16[8,1,8,4096]{3,2,0,1:T(8,128)(2,1)} reshape(bf16[8,8,32,128]{3,2,1,0:T(8,128)(2,1)} %get-tuple-element.4) | data formatting | bytes 1048576 | tf_op jit(solution)/shard_map/reshape | solution.py:331
  124.9 1.6 %reshape.120 = f32[1,8,4096]{2,1,0:T(8,128)} reshape(f32[1,8,32,128]{3,2,1,0:T(8,128)} %get-tuple-element.5) | data formatting | bytes 262144 | tf_op jit(solution)/shard_map/reshape | solution.py:331
  (11 shorter events, 0.1 us)
Async XLA Ops:
  7.2 3.2 %copy-start.1 = (bf16[8,1,4,4096]{3,2,1,0:T(4,128)(2,1)S(1)}, bf16[8,1,4,4096]{3,2,1,0:T(4,128)(2,1)}, u32[]{:S(2)}) copy-start(bf16[8,1,4,4096]{3,2,1,0:T(4,128)(2,1)} %param.8) | copy-start | bytes 786436
  7.2 4.2 %copy-start.3 = (s32[8,1,4]{0,2,1:T(4,128)S(1)}, s32[8,1,4]{0,2,1:T(4,128)}, u32[]{:S(2)}) copy-start(s32[8,1,4]{0,2,1:T(4,128)} %param.9) | copy-start | bytes 388
  7.2 20.2 %copy-start.2 = (s32[64,8]{0,1:T(8,128)S(1)}, s32[64,8]{0,1:T(8,128)}, u32[]{:S(2)}) copy-start(s32[64,8]{0,1:T(8,128)} %param.10) | copy-start | bytes 6148
  7.2 20.4 %copy-start.4 = (s32[32,8]{0,1:T(8,128)S(1)}, s32[32,8]{0,1:T(8,128)}, u32[]{:S(2)}) copy-start(s32[32,8]{0,1:T(8,128)} %param.11) | copy-start | bytes 3076
  7.2 21.6 %copy-start.5 = (s32[64,1,4]{0,2,1:T(4,128)S(1)}, s32[64,1,4]{0,2,1:T(4,128)}, u32[]{:S(2)}) copy-start(s32[64,1,4]{0,2,1:T(4,128)} %param.7) | copy-start | bytes 3076
  7.2 22.7 %copy-start = (bf16[64,1,4,4096]{3,2,1,0:T(4,128)(2,1)S(1)}, bf16[64,1,4,4096]{3,2,1,0:T(4,128)(2,1)}, u32[]{:S(2)}) copy-start(bf16[64,1,4,4096]{3,2,1,0:T(4,128)(2,1)} %param.6) | copy-start | bytes 6291460
  7.2 33.9 %all-gather.3.cloned.1.call-start = ((), (), s32[]{:S(2)}) async-start(), calls=%async_computation | async-start | bytes 1310720 | tf_op jit(solution)/shard_map/all_gather | solution.py:262
Sparse Core Ops, SparseCore 0:
  10.5 30.6 all-gather.2

commit v2 on v1

v2 whole, which is shorter than its diff:
```python
import functools

import jax
import jax.numpy as jnp
import numpy as np
from jax import lax
from jax.experimental import pallas as pl
from jax.experimental.pallas import tpu as pltpu
from jax.sharding import PartitionSpec as P

MESH = pl.DeviceIdType.MESH
F32 = jnp.float32
BF16 = jnp.bfloat16
LINK = jnp.int16
TOP = 32766.0


def left_mask(half):
    return lax.broadcasted_iota(jnp.int32, (half, 4 * half), 1) < 2 * half


def swap(x):
    return pltpu.roll(x, x.shape[1] // 2, 1)


def halves(x, left):
    other = swap(x)
    zero = jnp.zeros_like(x)
    in_left = jnp.concatenate([jnp.where(left, x, zero), jnp.where(left, other, zero)], axis=0)
    in_right = jnp.concatenate([jnp.where(left, zero, other), jnp.where(left, zero, x)], axis=0)
    return in_left.astype(BF16), in_right.astype(BF16)


def interleave(tile, left):
    half = left.shape[0]
    top, bottom = tile[:half], tile[half:]
    return jnp.where(left, top, swap(bottom)), jnp.where(left, swap(top), bottom)


def pack(value):
    most = jnp.maximum(jnp.max(jnp.abs(value), axis=0, keepdims=True), 1e-30)
    return jnp.round(value * (TOP / most)).astype(jnp.int32).astype(LINK), most * (1.0 / TOP)


def unpack(value, scale):
    return value.astype(jnp.int32).astype(F32) * scale


def gather_tiles(in_left, in_right, picks):
    return jnp.concatenate(
        [in_left[picks[n]] + in_right[picks[n + 1]] for n in range(0, len(picks), 2)], axis=1
    )


def turn_prolongator(left, pown_ref, order_ref, pt_l, pt_r, mine):
    order_mat = order_ref[...]
    contract = (((1,), (1,)), ((), ()))

    def body(n, carry):
        block = halves(pown_ref[n].astype(F32), left)[0]
        zero = jnp.zeros_like(block)
        for ref, pair in ((pt_l, [block, zero]), (pt_r, [zero, block])):
            ref[n] = lax.dot_general(
                order_mat, jnp.concatenate(pair, axis=0), contract, preferred_element_type=F32
            ).astype(BF16)
        return carry

    lax.fori_loop(0, mine, body, 0, unroll=2)
    pt_l[mine] = jnp.zeros(pt_l.shape[1:], BF16)
    pt_r[mine] = jnp.zeros(pt_r.shape[1:], BF16)


def kernel(
    sizes, a_ref, pnat_ref, pown_ref, order_ref, table_ref, fine_ref, kept_ref, pidx_ref, sidx_ref,
    ap_out, coarse_out,
    pg, tables, places, pl_l, pl_r, pt_l, pt_r, apl, apr,
    s1a, r1a, s2a, r2a, s1a_c, r1a_c, s2a_c, r2a_c, acc_a,
    s1b, r1b, s2b, r2b, s1b_c, r1b_c, s2b_c, r2b_c, acc_b, mine_b, s3, r3, s3_c, r3_c,
    up_send, up_recv, down_send, down_recv, table_send, table_recv, place_sem,
    s1a_send, s1a_recv, s2a_send, s2a_recv, s1b_send, s1b_recv, s2b_send, s2b_recv, s3_send, s3_recv,
):
    rows, cols, own, ka, kp, kap, kc, per, groups = sizes
    chips = cols // 2
    half = pnat_ref.shape[1]
    width = 2 * half
    left = left_mask(half)
    row, col = lax.axis_index("row"), lax.axis_index("col")
    core = lax.rem(col, 2)
    chip = col // 2
    partner = chip * 2 + 1 - core

    barrier = pltpu.get_barrier_semaphore()
    pl.semaphore_signal(barrier, inc=1, device_id=(row, partner), device_id_type=MESH)
    for d in range(1, chips):
        there = lax.rem(chip + d, chips) * 2 + core
        pl.semaphore_signal(barrier, inc=1, device_id=(row, there), device_id_type=MESH)
    for d in range(1, rows):
        pl.semaphore_signal(
            barrier, inc=1, device_id=(lax.rem(row + d, rows), col), device_id_type=MESH
        )

    mine = own * kp
    pl_l[groups] = jnp.zeros(pl_l.shape[1:], BF16)
    pl_r[groups] = jnp.zeros(pl_r.shape[1:], BF16)
    here = pl.ds(pl.multiple_of(row * own, own), own)
    tables[here, :] = table_ref[...]
    pl.semaphore_wait(barrier, chips + rows - 1)

    def up(h):
        shard = row - h
        return (shard >= 0) & (row + 1 < rows), pltpu.make_async_remote_copy(
            src_ref=pg.at[shard] if h else pnat_ref, dst_ref=pg.at[shard],
            send_sem=up_send.at[h], recv_sem=up_recv.at[h],
            device_id=(row + 1, col), device_id_type=MESH,
        )

    def down(h):
        shard = row + h
        return (shard < rows) & (row > 0), pltpu.make_async_remote_copy(
            src_ref=pg.at[shard] if h else pnat_ref, dst_ref=pg.at[shard],
            send_sem=down_send.at[h], recv_sem=down_recv.at[h],
            device_id=(row - 1, col), device_id_type=MESH,
        )

    def start(ready, copy):
        @pl.when(ready)
        def _():
            copy.start()

    def done_send(ready, copy):
        @pl.when(ready)
        def _():
            copy.wait_send()

    def spread(source, shard):
        def body(n, carry):
            in_left, in_right = halves(source[n].astype(F32), left)
            pl_l[shard * mine + n] = in_left
            pl_r[shard * mine + n] = in_right
            return carry

        lax.fori_loop(0, mine, body, 0, unroll=4)

    start(*up(0))
    start(*down(0))
    table_copies = []
    for d in range(1, rows):
        copy = pltpu.make_async_remote_copy(
            src_ref=tables.at[here], dst_ref=tables.at[here],
            send_sem=table_send.at[d - 1], recv_sem=table_recv.at[d - 1],
            device_id=(lax.rem(row + d, rows), col), device_id_type=MESH,
        )
        copy.start()
        table_copies.append(copy)
    spread(pnat_ref, row)
    turn_prolongator(left, pown_ref, order_ref, pt_l, pt_r, mine)
    for copy in table_copies:
        copy.wait()
    to_smem = pltpu.make_async_copy(tables, places, place_sem)
    to_smem.start()
    for h in range(rows - 1):
        @pl.when(row - 1 - h >= 0)
        def _():
            up(h)[1].wait_recv()

        if h + 1 < rows - 1:
            start(*up(h + 1))

        @pl.when(row + 1 + h < rows)
        def _():
            down(h)[1].wait_recv()

        if h + 1 < rows - 1:
            start(*down(h + 1))

        @pl.when(row - 1 - h >= 0)
        def _():
            spread(pg.at[row - 1 - h], row - 1 - h)

        @pl.when(row + 1 + h < rows)
        def _():
            spread(pg.at[row + 1 + h], row + 1 + h)

    to_smem.wait()

    def product_row(to, u):
        i = u * cols + to
        lhs = []
        for e in range(0, ka, 2):
            x0, x1 = a_ref[i, e].astype(F32), a_ref[i, e + 1].astype(F32)
            top = jnp.where(left, x0, swap(x1))
            bottom = jnp.where(left, swap(x0), x1)
            lhs.append(jnp.concatenate([top, bottom], axis=0).astype(BF16))
        kept = [kept_ref[i * kap + s] for s in range(kap)]
        fine = [fine_ref[i * ka + e] for e in range(ka)]
        rhs = [gather_tiles(pl_l, pl_r, [places[k, j] for j in kept]) for k in fine]
        return jnp.dot(
            jnp.concatenate(lhs, axis=1), jnp.concatenate(rhs, axis=0), preferred_element_type=F32
        )

    def coarse_row(to, n):
        j = ((n // per) * cols + to) * per + lax.rem(n, per)
        lhs = gather_tiles(pt_l, pt_r, [pidx_ref[j * own + u] for u in range(own)])
        rhs = [
            gather_tiles(apl, apr, [sidx_ref[(j * own + u) * kc + t] for t in range(kc)])
            for u in range(own)
        ]
        return jnp.dot(lhs, jnp.concatenate(rhs, axis=0), preferred_element_type=F32)

    def reduce_plane(compute, count, bufs, acc, sems):
        s1, r1, s2, r2, s1_c, r1_c, s2_c, r2_c = bufs
        s1_send, s1_recv, s2_send, s2_recv = sems
        order = list(range(1, chips)) + [0]
        first, second = [], []

        def give(n):
            d = order[n]
            to = lax.rem(chip + d, chips) * 2 + 1 - core
            slot = n % s1.shape[0]
            if n >= s1.shape[0]:
                for copy in first[n - s1.shape[0]]:
                    copy.wait_send()

            def body(k, carry):
                s1[slot, k], s1_c[slot, pl.ds(k, 1), :] = pack(compute(to, k))
                return carry

            lax.fori_loop(0, count, body, 0)
            copies = [
                pltpu.make_async_remote_copy(
                    src_ref=src.at[slot], dst_ref=dst.at[n], send_sem=s1_send.at[w, n], recv_sem=s1_recv.at[w, n],
                    device_id=(row, partner), device_id_type=MESH,
                )
                for w, (src, dst) in enumerate(((s1, r1), (s1_c, r1_c)))
            ]
            for copy in copies:
                copy.start()
            first.append(copies)

        def finish(n):
            d = order[n]
            to = lax.rem(chip + d, chips) * 2 + core
            slot = n % s2.shape[0]
            for copy in first[n]:
                copy.wait_recv()
            if d and n >= s2.shape[0]:
                for copy in second[n - s2.shape[0]]:
                    copy.wait_send()

            def body(k, carry):
                value = compute(to, k) + unpack(r1[n, k], r1_c[n, pl.ds(k, 1), :])
                if d:
                    s2[slot, k], s2_c[slot, pl.ds(k, 1), :] = pack(value)
                else:
                    acc[k] = value
                return carry

            lax.fori_loop(0, count, body, 0)
            if d:
                copies = [
                    pltpu.make_async_remote_copy(
                        src_ref=src.at[slot], dst_ref=dst.at[n], send_sem=s2_send.at[w, n], recv_sem=s2_recv.at[w, n],
                        device_id=(row, to), device_id_type=MESH,
                    )
                    for w, (src, dst) in enumerate(((s2, r2), (s2_c, r2_c)))
                ]
                for copy in copies:
                    copy.start()
                second.append(copies)

        for n in range(chips):
            give(n)
            if n:
                finish(n - 1)
        finish(chips - 1)
        for n in range(max(0, chips - s1.shape[0]), chips):
            for copy in first[n]:
                copy.wait_send()
        for copies in second:
            for copy in copies:
                copy.wait_recv()
        for n in range(max(0, chips - 1 - s2.shape[0]), chips - 1):
            for copy in second[n]:
                copy.wait_send()

        def total(k):
            value = acc[k]
            for n in range(chips - 1):
                value = value + unpack(r2[n, k], r2_c[n, pl.ds(k, 1), :])
            return value

        return total

    total = reduce_plane(
        product_row, own, (s1a, r1a, s2a, r2a, s1a_c, r1a_c, s2a_c, r2a_c), acc_a,
        (s1a_send, s1a_recv, s2a_send, s2a_recv),
    )

    def keep(u, carry):
        value = total(u).astype(BF16).astype(F32)
        for s in range(0, kap, 2):
            tile = value[:, s * width : (s + 2) * width]
            x0, x1 = interleave(tile, left)
            ap_out[u, s] = x0.astype(BF16)
            ap_out[u, s + 1] = x1.astype(BF16)
            for n, x in ((s, x0), (s + 1, x1)):
                in_left, in_right = halves(x, left)
                apl[u * kap + n] = in_left
                apr[u * kap + n] = in_right
        return carry

    lax.fori_loop(0, own, keep, 0)
    apl[own * kap] = jnp.zeros(apl.shape[1:], BF16)
    apr[own * kap] = jnp.zeros(apr.shape[1:], BF16)

    coarse_total = reduce_plane(
        coarse_row, rows * per, (s1b, r1b, s2b, r2b, s1b_c, r1b_c, s2b_c, r2b_c), acc_b,
        (s1b_send, s1b_recv, s2b_send, s2b_recv),
    )
    third = []
    for d in list(range(1, rows)) + [0]:
        to = lax.rem(row + d, rows)
        for q in range(per):
            value = coarse_total(to * per + q)
            if d:
                s3[d - 1, q], s3_c[d - 1, pl.ds(q, 1), :] = pack(value)
            else:
                mine_b[q] = value
        if d:
            for w, (src, dst) in enumerate(((s3, r3), (s3_c, r3_c))):
                copy = pltpu.make_async_remote_copy(
                    src_ref=src.at[d - 1], dst_ref=dst.at[d - 1],
                    send_sem=s3_send.at[w, d - 1], recv_sem=s3_recv.at[w, d - 1],
                    device_id=(to, col), device_id_type=MESH,
                )
                copy.start()
                third.append(copy)
    for copy in third:
        copy.wait()
    for q in range(per):
        value = mine_b[q]
        for d in range(1, rows):
            value = value + unpack(r3[d - 1, q], r3_c[d - 1, pl.ds(q, 1), :])
        for t in range(0, kc, 2):
            x0, x1 = interleave(value[:, t * width : (t + 2) * width], left)
            coarse_out[q, t] = x0
            coarse_out[q, t + 1] = x1
    for h in range(rows - 1):
        done_send(*up(h))
        done_send(*down(h))


def shards(a_blocks, a_index, p_blocks, p_index, ap_index, coarse_index):
    rows, cols = lax.axis_size("row"), lax.axis_size("col")
    count, _, ka, flat = a_blocks.shape
    own, _, kp, _ = p_blocks.shape
    kap = ap_index.shape[1]
    coarse, kc = coarse_index.shape
    per = coarse // (rows * cols)
    width = int(round(flat ** 0.5))
    half = width // 2
    lanes = 2 * width

    a2 = a_blocks.reshape(count, ka, half, lanes)
    p2 = p_blocks.reshape(own * kp, half, lanes)
    p_nat = p_blocks.reshape(own * kp, 2, half, width).transpose(0, 2, 1, 3).reshape(own * kp, half, lanes)
    groups = rows * own * kp
    across = -(-coarse // 128) * 128

    mine = p_index[:, 0]
    slots = lax.dynamic_index_in_dim(ap_index.reshape(own, cols, kap), lax.axis_index("col"), 1, keepdims=False)
    which = jnp.arange(own * kp, dtype=jnp.int32).reshape(own, kp)
    hit = mine[None] == jnp.arange(coarse, dtype=jnp.int32)[:, None, None]
    p_pick = jnp.where(jnp.any(hit, axis=2), jnp.sum(jnp.where(hit, which[None], 0), axis=2), own * kp)
    here = lax.axis_index("row") * (own * kp) + which
    sits = mine[:, :, None] == lax.broadcasted_iota(jnp.int32, (1, 1, across), 2)
    table = jnp.where(jnp.any(sits, axis=1), jnp.sum(jnp.where(sits, here[:, :, None], 0), axis=1), groups)
    spot = jnp.arange(own * kap, dtype=jnp.int32).reshape(own, kap)
    match = coarse_index[:, None, :, None] == slots[None, :, None, :]
    s_pick = jnp.where(
        jnp.any(match, axis=3), jnp.sum(jnp.where(match, spot[None, :, None, :], 0), axis=3), own * kap
    )

    into = np.arange(width)
    source = (into % half) * 2 + into // half
    order_mat = jnp.asarray(source[:, None] == np.arange(lanes)[None, :], BF16)

    chips = cols // 2
    others = max(chips - 1, 1)
    slots2 = min(others, 3)
    wide = kap * width
    wide_c = kc * width
    vmem = pl.BlockSpec(memory_space=pltpu.VMEM)
    smem = pl.BlockSpec(memory_space=pltpu.SMEM)
    dma = pltpu.SemaphoreType.DMA
    n_coarse = rows * per
    beyond = max(rows - 1, 1)

    def sums(n, across_lanes):
        depths = (2, chips, slots2, others)
        return [
            *[pltpu.VMEM((k, n, width, across_lanes), LINK) for k in depths],
            *[pltpu.VMEM((k, n, across_lanes), F32) for k in depths],
            pltpu.VMEM((n, width, across_lanes), F32),
        ]

    ap, coarse_out = pl.pallas_call(
        functools.partial(kernel, (rows, cols, own, ka, kp, kap, kc, per, groups)),
        out_shape=(
            jax.ShapeDtypeStruct((own, kap, half, lanes), BF16),
            jax.ShapeDtypeStruct((per, kc, half, lanes), F32),
        ),
        in_specs=[vmem, vmem, vmem, vmem, vmem, smem, smem, smem, smem],
        out_specs=(vmem, vmem),
        scratch_shapes=[
            pltpu.VMEM((rows, own * kp, half, lanes), BF16),
            pltpu.VMEM((rows * own, across), jnp.int32),
            pltpu.SMEM((rows * own, across), jnp.int32),
            pltpu.VMEM((groups + 1, width, lanes), BF16),
            pltpu.VMEM((groups + 1, width, lanes), BF16),
            pltpu.VMEM((own * kp + 1, width, lanes), BF16),
            pltpu.VMEM((own * kp + 1, width, lanes), BF16),
            pltpu.VMEM((own * kap + 1, width, lanes), BF16),
            pltpu.VMEM((own * kap + 1, width, lanes), BF16),
            *sums(own, wide),
            *sums(n_coarse, wide_c),
            pltpu.VMEM((per, width, wide_c), F32),
            pltpu.VMEM((beyond, per, width, wide_c), LINK),
            pltpu.VMEM((beyond, per, width, wide_c), LINK),
            pltpu.VMEM((beyond, per, wide_c), F32),
            pltpu.VMEM((beyond, per, wide_c), F32),
            dma((beyond,)), dma((beyond,)), dma((beyond,)), dma((beyond,)), dma((beyond,)), dma((beyond,)), dma,
            dma((2, chips)), dma((2, chips)), dma((2, others)), dma((2, others)),
            dma((2, chips)), dma((2, chips)), dma((2, others)), dma((2, others)),
            dma((2, beyond)), dma((2, beyond)),
        ],
        compiler_params=pltpu.CompilerParams(
            collective_id=0, has_side_effects=True, vmem_limit_bytes=60 * 1024 * 1024
        ),
    )(a2, p_nat, p2, order_mat, table, a_index.reshape(-1), ap_index.reshape(-1), p_pick.reshape(-1), s_pick.reshape(-1))
    return ap.reshape(own, 1, kap, flat), coarse_out.reshape(per, kc, flat)


def solution(mesh):
    placed = (
        P("row", "col", None, None),
        P("row", "col", None),
        P("row", "col", None, None),
        P("row", "col", None),
        P("row", None),
        P(),
    )
    return jax.shard_map(
        shards,
        mesh=mesh,
        in_specs=placed,
        out_specs=(P("row", "col", None, None), P(("row", "col"), None, None)),
        check_vma=False,
    )
```

time: 135 us -> 113 us (0.84)
  blocking collectives: 14.9 us -> 0 us
  between operations: 14.2 us -> 0.72 us
  waiting for transfers between devices: 7.35 us -> 0 us
  Pallas kernels: 81.7 us -> 88.4 us
  other arithmetic: 1.37 us -> 5.51 us
  local copies, waits for them, and re-layouts: 13.8 us -> 17.1 us
    all_gather x1 -> x0, blocking collectives: 14.9 us -> none  [shards(): group_cols = lax.all_gather(p_index[:, 0], 'row', axis=0, tiled=True)]
    all_gather x1 -> x0, waiting for transfers between devices: 7.33 us -> none  [shards(): group = lax.all_gather(p_nat, 'row', axis=0, tiled=True)]
    pallas_call x1, Pallas kernels: 81.7 us -> 88.4 us  [shards(): pl.pallas_call(functools.partial(kernel, (rows, cols, own, ka, kp, kap, k...]
    unnamed x13 -> x4, local copies, waits for them, and re-layouts: 0.11 us -> 1.55 us
  transfers between devices with their start and end apart: 1 -> 0, of which waited for: 1 -> 0; matrix products, arithmetic and copies ran while one was open for 6% -> 0% of each run, Pallas kernels for 0% -> 0%
where the time goes in v2:
time: 113 us; the launch traced here: 112 us
  Pallas kernels  88.4 us (78%)
  local copies, waits for them, and re-layouts  17.1 us (15%)
  other arithmetic  5.51 us (5%)
    pallas_call x1, Pallas kernels, shards(): pl.pallas_call(functools.partial(kernel, (rows, cols, own, ka, kp, kap, k...  88.4 us
    reshape x2, local copies, waits for them, and re-layouts, shards(): return (ap.reshape(own, 1, kap, flat), coarse_out.reshape(per, kc, flat))  3.65 us
    reshape x1, local copies, waits for them, and re-layouts, shards(): a2 = a_blocks.reshape(count, ka, half, lanes)  3.25 us
    reshape x3, local copies, waits for them, and re-layouts, shards(): p_blocks.reshape(own * kp, 2, half, width).transpose(0, 2, 1, 3)  2.88 us

profile of v2, /device:TPU:0, one launch (start us, length us, event | category | flops | bytes accessed | tf_op | source)
XLA Modules:
  0.0 111.8 jit_solution(15223053057145485463)
XLA Ops:
  0.6 0.0 copy-start
  0.6 0.9 fusion.1
  1.6 0.8 fusion.2
  2.3 0.8 select_reduce_fusion.1
  3.1 0.6 broadcast_select_fusion.2.table_ref
  3.7 0.8 select_reduce_fusion
  4.5 0.1 copy.25
  4.5 0.7 select_n.40.pidx_ref
  5.2 0.8 copy.23
  6.0 0.7 reshape.96.fine_ref
  6.7 0.8 reshape.98
  7.4 0.1 constant_dynamic-slice_fusion
  7.5 0.1 copy.26
  7.6 0.9 compare_reduce_fusion
  8.5 0.8 fusion
  9.4 0.8 copy.24
  10.1 0.6 reshape.97.kept_ref
  10.8 0.1 copy.27
  10.9 0.7 select_n.44.sidx_ref
  11.6 1.9 %reshape.92.pown_ref = bf16[32,32,128]{2,1,0:T(8,128)(2,1)} reshape(bf16[8,1,4,4096]{3,2,1,0:T(4,128)(2,1)} %param.9) | data formatting | bytes 524288 | tf_op jit(solution)/shard_map/reshape | solution.py:365
  13.5 1.4 %reshape.90 = bf16[32,2,32,64]{3,2,1,0:T(8,128)(2,1)S(1)} reshape(bf16[8,1,4,4096]{3,2,1,0:T(4,128)(2,1)} %param.9) | data formatting | bytes 524288 | tf_op jit(solution)/shard_map/reshape | solution.py:366
  15.0 0.5 copy.30
  15.5 1.0 reshape.91.pnat_ref
  16.4 0.0 copy-done
  16.4 3.3 %reshape.89.a_ref = bf16[64,4,32,128]{3,2,1,0:T(8,128)(2,1)} reshape(bf16[64,1,4,4096]{3,2,1,0:T(4,128)(2,1)S(1)} %copy-done) | data formatting | bytes 4194304 | tf_op jit(solution)/shard_map/reshape | solution.py:364
  19.7 88.4 %shard_map.86 = (bf16[8,8,32,128]{3,2,1,0:T(8,128)(2,1)}, f32[1,8,32,128]{3,2,1,0:T(8,128)}) custom-call(bf16[64,4,32,128]{3,2,1,0:T(8,128)(2,1)} %reshape.89.a_ref, bf16[32,32,128]{2,1,0:T(8,128)(2,1)} %reshape.91.pnat_ref, bf16[32,32,128]{2,1,0:T(8,128)(2,1)} %reshape.92.pown_ref, bf16[64,128]{1,0:T(8,128)(2,1)} %constant.31.clone.order_ref, ...), custom_call_target="tpu_custom_call" | custom-call | tf_op jit(solution)/shard_map/pallas_call | solution.py:407
  108.1 2.1 %reshape.99 = bf16[8,1,8,4096]{3,2,0,1:T(8,128)(2,1)} reshape(bf16[8,8,32,128]{3,2,1,0:T(8,128)(2,1)} %get-tuple-element.4) | data formatting | bytes 1048576 | tf_op jit(solution)/shard_map/reshape | solution.py:441
  110.2 1.6 %reshape.100 = f32[1,8,4096]{2,1,0:T(8,128)} reshape(f32[1,8,32,128]{3,2,1,0:T(8,128)} %get-tuple-element.5) | data formatting | bytes 262144 | tf_op jit(solution)/shard_map/reshape | solution.py:441
  (5 shorter events, 0.0 us)
Async XLA Ops:
  0.6 15.8 %copy-start = (bf16[64,1,4,4096]{3,2,1,0:T(4,128)(2,1)S(1)}, bf16[64,1,4,4096]{3,2,1,0:T(4,128)(2,1)}, u32[]{:S(2)}) copy-start(bf16[64,1,4,4096]{3,2,1,0:T(4,128)(2,1)} %param.7) | copy-start | bytes 6291460

commit v3 on v2

--- a/solution.py
+++ b/solution.py
@@ -2,7 +2,6 @@
 
 import jax
 import jax.numpy as jnp
-import numpy as np
 from jax import lax
 from jax.experimental import pallas as pl
 from jax.experimental.pallas import tpu as pltpu
@@ -52,12 +51,15 @@
     )
 
 
-def turn_prolongator(left, pown_ref, order_ref, pt_l, pt_r, mine):
-    order_mat = order_ref[...]
+def turn_prolongator(left, own_ref, pt_l, pt_r, mine):
+    half, lanes = left.shape
+    into = lax.broadcasted_iota(jnp.int32, (2 * half, lanes), 0)
+    source = lax.rem(into, half) * 2 + into // half
+    order_mat = (source == lax.broadcasted_iota(jnp.int32, (2 * half, lanes), 1)).astype(F32).astype(BF16)
     contract = (((1,), (1,)), ((), ()))
 
     def body(n, carry):
-        block = halves(pown_ref[n].astype(F32), left)[0]
+        block = halves(own_ref[n].astype(F32), left)[0]
         zero = jnp.zeros_like(block)
         for ref, pair in ((pt_l, [block, zero]), (pt_r, [zero, block])):
             ref[n] = lax.dot_general(
@@ -65,15 +67,26 @@
             ).astype(BF16)
         return carry
 
-    lax.fori_loop(0, mine, body, 0, unroll=2)
+    lax.fori_loop(0, mine, body, 0, unroll=4)
     pt_l[mine] = jnp.zeros(pt_l.shape[1:], BF16)
     pt_r[mine] = jnp.zeros(pt_r.shape[1:], BF16)
 
 
+def to_rows(flat, out, half):
+    n, lanes = flat.shape[0], out.shape[1]
+    for j in range(half):
+        out[pl.ds(j, n, stride=half), :] = flat[:, j * lanes : (j + 1) * lanes]
+
+
+def to_flat(rows_ref, n, half, j):
+    return rows_ref[pl.ds(j, n, stride=half), :]
+
+
 def kernel(
-    sizes, a_ref, pnat_ref, pown_ref, order_ref, table_ref, fine_ref, kept_ref, pidx_ref, sidx_ref,
+    sizes, a_ref, p_ref, fine_ref, pcol_ref, kept_ref, cols_ref,
     ap_out, coarse_out,
-    pg, tables, places, pl_l, pl_r, pt_l, pt_r, apl, apr,
+    a_pre, pg, tables, local, spots, places, local_places, spot_places, rows_in, rows_out,
+    pl_l, pl_r, pt_l, pt_r, apl, apr,
     s1a, r1a, s2a, r2a, s1a_c, r1a_c, s2a_c, r2a_c, acc_a,
     s1b, r1b, s2b, r2b, s1b_c, r1b_c, s2b_c, r2b_c, acc_b, mine_b, s3, r3, s3_c, r3_c,
     up_send, up_recv, down_send, down_recv, table_send, table_recv, place_sem,
@@ -81,7 +94,7 @@
 ):
     rows, cols, own, ka, kp, kap, kc, per, groups = sizes
     chips = cols // 2
-    half = pnat_ref.shape[1]
+    half = pg.shape[2]
     width = 2 * half
     left = left_mask(half)
     row, col = lax.axis_index("row"), lax.axis_index("col")
@@ -100,16 +113,37 @@
         )
 
     mine = own * kp
+
+    def lay_out(u, carry):
+        to_rows(p_ref[u, 0].astype(F32), rows_in.at[0], half)
+        for m in range(kp):
+            pg[row, u * kp + m] = rows_in[0, m * half : (m + 1) * half, :].astype(BF16)
+        return carry
+
+    lax.fori_loop(0, own, lay_out, 0)
+    lane = lax.broadcasted_iota(jnp.int32, (1, tables.shape[1]), 1)
+    lines = []
+    for u in range(own):
+        line = jnp.full(lane.shape, mine, jnp.int32)
+        for m in range(kp):
+            line = jnp.where(lane == pcol_ref[u, 0, m], u * kp + m, line)
+        lines.append(line)
+        spot = jnp.full(lane.shape, own * kap, jnp.int32)
+        for n in range(kap):
+            spot = jnp.where(lane == kept_ref[u * cols + col, n], u * kap + n, spot)
+        spots[u : u + 1, :] = spot
+    lines = jnp.concatenate(lines, axis=0)
+    local[...] = lines
+    here = pl.ds(pl.multiple_of(row * own, own), own)
+    tables[here, :] = jnp.where(lines < mine, lines + row * mine, groups)
     pl_l[groups] = jnp.zeros(pl_l.shape[1:], BF16)
     pl_r[groups] = jnp.zeros(pl_r.shape[1:], BF16)
-    here = pl.ds(pl.multiple_of(row * own, own), own)
-    tables[here, :] = table_ref[...]
     pl.semaphore_wait(barrier, chips + rows - 1)
 
     def up(h):
         shard = row - h
         return (shard >= 0) & (row + 1 < rows), pltpu.make_async_remote_copy(
-            src_ref=pg.at[shard] if h else pnat_ref, dst_ref=pg.at[shard],
+            src_ref=pg.at[shard], dst_ref=pg.at[shard],
             send_sem=up_send.at[h], recv_sem=up_recv.at[h],
             device_id=(row + 1, col), device_id_type=MESH,
         )
@@ -117,7 +151,7 @@
     def down(h):
         shard = row + h
         return (shard < rows) & (row > 0), pltpu.make_async_remote_copy(
-            src_ref=pg.at[shard] if h else pnat_ref, dst_ref=pg.at[shard],
+            src_ref=pg.at[shard], dst_ref=pg.at[shard],
             send_sem=down_send.at[h], recv_sem=down_recv.at[h],
             device_id=(row - 1, col), device_id_type=MESH,
         )
@@ -132,11 +166,16 @@
         def _():
             copy.wait_send()
 
-    def spread(source, shard):
+    into = lax.broadcasted_iota(jnp.int32, (width, width), 0)
+    natural = lax.rem(into, 2) * half + into // 2 == lax.broadcasted_iota(jnp.int32, (width, width), 1)
+    natural = natural.astype(F32).astype(BF16)
+
+    def spread(shard):
         def body(n, carry):
-            in_left, in_right = halves(source[n].astype(F32), left)
-            pl_l[shard * mine + n] = in_left
-            pl_r[shard * mine + n] = in_right
+            pair = jnp.concatenate(halves(pg[shard, n].astype(F32), left), axis=1)
+            pair = jnp.dot(natural, pair, preferred_element_type=F32).astype(BF16)
+            pl_l[shard * mine + n] = pair[:, : 2 * width]
+            pl_r[shard * mine + n] = pair[:, 2 * width :]
             return carry
 
         lax.fori_loop(0, mine, body, 0, unroll=4)
@@ -152,12 +191,33 @@
         )
         copy.start()
         table_copies.append(copy)
-    spread(pnat_ref, row)
-    turn_prolongator(left, pown_ref, order_ref, pt_l, pt_r, mine)
+    small = [
+        pltpu.make_async_copy(local, local_places, place_sem.at[0]),
+        pltpu.make_async_copy(spots, spot_places, place_sem.at[1]),
+    ]
+    for copy in small:
+        copy.start()
+
+    def lay_rows(n, carry):
+        for k in range(2):
+            i = n * 2 + k
+            to_rows(a_ref[i, 0].astype(F32), rows_in.at[k], half)
+            for e in range(0, ka, 2):
+                x0 = rows_in[k, e * half : (e + 1) * half, :]
+                x1 = rows_in[k, (e + 1) * half : (e + 2) * half, :]
+                top = jnp.where(left, x0, swap(x1))
+                bottom = jnp.where(left, swap(x0), x1)
+                tile = jnp.concatenate([top, bottom], axis=0).astype(BF16)
+                a_pre[i, :, e * width : (e + 2) * width] = tile
+        return carry
+
+    lax.fori_loop(0, a_ref.shape[0] // 2, lay_rows, 0)
+    spread(row)
+    turn_prolongator(left, pg.at[row], pt_l, pt_r, mine)
     for copy in table_copies:
         copy.wait()
-    to_smem = pltpu.make_async_copy(tables, places, place_sem)
-    to_smem.start()
+    small.append(pltpu.make_async_copy(tables, places, place_sem.at[2]))
+    small[2].start()
     for h in range(rows - 1):
         @pl.when(row - 1 - h >= 0)
         def _():
@@ -175,36 +235,27 @@
 
         @pl.when(row - 1 - h >= 0)
         def _():
-            spread(pg.at[row - 1 - h], row - 1 - h)
+            spread(row - 1 - h)
 
         @pl.when(row + 1 + h < rows)
         def _():
-            spread(pg.at[row + 1 + h], row + 1 + h)
-
-    to_smem.wait()
+            spread(row + 1 + h)
+
+    for copy in small:
+        copy.wait()
 
     def product_row(to, u):
         i = u * cols + to
-        lhs = []
-        for e in range(0, ka, 2):
-            x0, x1 = a_ref[i, e].astype(F32), a_ref[i, e + 1].astype(F32)
-            top = jnp.where(left, x0, swap(x1))
-            bottom = jnp.where(left, swap(x0), x1)
-            lhs.append(jnp.concatenate([top, bottom], axis=0).astype(BF16))
-        kept = [kept_ref[i * kap + s] for s in range(kap)]
-        fine = [fine_ref[i * ka + e] for e in range(ka)]
+        kept = [kept_ref[i, n] for n in range(kap)]
+        fine = [fine_ref[i, 0, e] for e in range(ka)]
         rhs = [gather_tiles(pl_l, pl_r, [places[k, j] for j in kept]) for k in fine]
-        return jnp.dot(
-            jnp.concatenate(lhs, axis=1), jnp.concatenate(rhs, axis=0), preferred_element_type=F32
-        )
+        return jnp.dot(a_pre[i], jnp.concatenate(rhs, axis=0), preferred_element_type=F32)
 
     def coarse_row(to, n):
         j = ((n // per) * cols + to) * per + lax.rem(n, per)
-        lhs = gather_tiles(pt_l, pt_r, [pidx_ref[j * own + u] for u in range(own)])
-        rhs = [
-            gather_tiles(apl, apr, [sidx_ref[(j * own + u) * kc + t] for t in range(kc)])
-            for u in range(own)
-        ]
+        lhs = gather_tiles(pt_l, pt_r, [local_places[u, j] for u in range(own)])
+        kept = [cols_ref[j, t] for t in range(kc)]
+        rhs = [gather_tiles(apl, apr, [spot_places[u, c] for c in kept]) for u in range(own)]
         return jnp.dot(lhs, jnp.concatenate(rhs, axis=0), preferred_element_type=F32)
 
     def reduce_plane(compute, count, bufs, acc, sems):
@@ -225,7 +276,7 @@
                 s1[slot, k], s1_c[slot, pl.ds(k, 1), :] = pack(compute(to, k))
                 return carry
 
-            lax.fori_loop(0, count, body, 0)
+            lax.fori_loop(0, count, body, 0, unroll=2)
             copies = [
                 pltpu.make_async_remote_copy(
                     src_ref=src.at[slot], dst_ref=dst.at[n], send_sem=s1_send.at[w, n], recv_sem=s1_recv.at[w, n],
@@ -255,7 +306,7 @@
                     acc[k] = value
                 return carry
 
-            lax.fori_loop(0, count, body, 0)
+            lax.fori_loop(0, count, body, 0, unroll=2)
             if d:
                 copies = [
                     pltpu.make_async_remote_copy(
@@ -301,12 +352,14 @@
         for s in range(0, kap, 2):
             tile = value[:, s * width : (s + 2) * width]
             x0, x1 = interleave(tile, left)
-            ap_out[u, s] = x0.astype(BF16)
-            ap_out[u, s + 1] = x1.astype(BF16)
+            rows_out[s * half : (s + 1) * half, :] = x0
+            rows_out[(s + 1) * half : (s + 2) * half, :] = x1
             for n, x in ((s, x0), (s + 1, x1)):
                 in_left, in_right = halves(x, left)
                 apl[u * kap + n] = in_left
                 apr[u * kap + n] = in_right
+        for j in range(half):
+            ap_out[u, 0, :, j * 2 * width : (j + 1) * 2 * width] = to_flat(rows_out, kap, half, j).astype(BF16)
         return carry
 
     lax.fori_loop(0, own, keep, 0)
@@ -343,8 +396,10 @@
             value = value + unpack(r3[d - 1, q], r3_c[d - 1, pl.ds(q, 1), :])
         for t in range(0, kc, 2):
             x0, x1 = interleave(value[:, t * width : (t + 2) * width], left)
-            coarse_out[q, t] = x0
-            coarse_out[q, t + 1] = x1
+            rows_out[t * half : (t + 1) * half, :] = x0
+            rows_out[(t + 1) * half : (t + 2) * half, :] = x1
+        for j in range(half):
+            coarse_out[q, :, j * 2 * width : (j + 1) * 2 * width] = to_flat(rows_out, kc, half, j)
     for h in range(rows - 1):
         done_send(*up(h))
         done_send(*down(h))
@@ -361,30 +416,8 @@
     half = width // 2
     lanes = 2 * width
 
-    a2 = a_blocks.reshape(count, ka, half, lanes)
-    p2 = p_blocks.reshape(own * kp, half, lanes)
-    p_nat = p_blocks.reshape(own * kp, 2, half, width).transpose(0, 2, 1, 3).reshape(own * kp, half, lanes)
     groups = rows * own * kp
     across = -(-coarse // 128) * 128
-
-    mine = p_index[:, 0]
-    slots = lax.dynamic_index_in_dim(ap_index.reshape(own, cols, kap), lax.axis_index("col"), 1, keepdims=False)
-    which = jnp.arange(own * kp, dtype=jnp.int32).reshape(own, kp)
-    hit = mine[None] == jnp.arange(coarse, dtype=jnp.int32)[:, None, None]
-    p_pick = jnp.where(jnp.any(hit, axis=2), jnp.sum(jnp.where(hit, which[None], 0), axis=2), own * kp)
-    here = lax.axis_index("row") * (own * kp) + which
-    sits = mine[:, :, None] == lax.broadcasted_iota(jnp.int32, (1, 1, across), 2)
-    table = jnp.where(jnp.any(sits, axis=1), jnp.sum(jnp.where(sits, here[:, :, None], 0), axis=1), groups)
-    spot = jnp.arange(own * kap, dtype=jnp.int32).reshape(own, kap)
-    match = coarse_index[:, None, :, None] == slots[None, :, None, :]
-    s_pick = jnp.where(
-        jnp.any(match, axis=3), jnp.sum(jnp.where(match, spot[None, :, None, :], 0), axis=3), own * kap
-    )
-
-    into = np.arange(width)
-    source = (into % half) * 2 + into // half
-    order_mat = jnp.asarray(source[:, None] == np.arange(lanes)[None, :], BF16)
-
     chips = cols // 2
     others = max(chips - 1, 1)
     slots2 = min(others, 3)
@@ -407,15 +440,22 @@
     ap, coarse_out = pl.pallas_call(
         functools.partial(kernel, (rows, cols, own, ka, kp, kap, kc, per, groups)),
         out_shape=(
-            jax.ShapeDtypeStruct((own, kap, half, lanes), BF16),
-            jax.ShapeDtypeStruct((per, kc, half, lanes), F32),
+            jax.ShapeDtypeStruct((own, 1, kap, flat), BF16),
+            jax.ShapeDtypeStruct((per, kc, flat), F32),
         ),
-        in_specs=[vmem, vmem, vmem, vmem, vmem, smem, smem, smem, smem],
+        in_specs=[vmem, vmem, smem, smem, smem, smem],
         out_specs=(vmem, vmem),
         scratch_shapes=[
+            pltpu.VMEM((count, width, ka * width), BF16),
             pltpu.VMEM((rows, own * kp, half, lanes), BF16),
             pltpu.VMEM((rows * own, across), jnp.int32),
+            pltpu.VMEM((own, across), jnp.int32),
+            pltpu.VMEM((own, across), jnp.int32),
             pltpu.SMEM((rows * own, across), jnp.int32),
+            pltpu.SMEM((own, across), jnp.int32),
+            pltpu.SMEM((own, across), jnp.int32),
+            pltpu.VMEM((2, max(ka, kp) * half, lanes), F32),
+            pltpu.VMEM((max(kap, kc) * half, lanes), F32),
             pltpu.VMEM((groups + 1, width, lanes), BF16),
             pltpu.VMEM((groups + 1, width, lanes), BF16),
             pltpu.VMEM((own * kp + 1, width, lanes), BF16),
@@ -429,7 +469,7 @@
             pltpu.VMEM((beyond, per, width, wide_c), LINK),
             pltpu.VMEM((beyond, per, wide_c), F32),
             pltpu.VMEM((beyond, per, wide_c), F32),
-            dma((beyond,)), dma((beyond,)), dma((beyond,)), dma((beyond,)), dma((beyond,)), dma((beyond,)), dma,
+            dma((beyond,)), dma((beyond,)), dma((beyond,)), dma((beyond,)), dma((beyond,)), dma((beyond,)), dma((3,)),
             dma((2, chips)), dma((2, chips)), dma((2, others)), dma((2, others)),
             dma((2, chips)), dma((2, chips)), dma((2, others)), dma((2, others)),
             dma((2, beyond)), dma((2, beyond)),
@@ -437,8 +477,8 @@
         compiler_params=pltpu.CompilerParams(
             collective_id=0, has_side_effects=True, vmem_limit_bytes=60 * 1024 * 1024
         ),
-    )(a2, p_nat, p2, order_mat, table, a_index.reshape(-1), ap_index.reshape(-1), p_pick.reshape(-1), s_pick.reshape(-1))
-    return ap.reshape(own, 1, kap, flat), coarse_out.reshape(per, kc, flat)
+    )(a_blocks, p_blocks, a_index, p_index, ap_index, coarse_index)
+    return ap, coarse_out
 
 
 def solution(mesh):

time: 113 us -> 101 us (0.89)
  local copies, waits for them, and re-layouts: 17.1 us -> 8.9 us
  other arithmetic: 5.51 us -> 0 us
  Pallas kernels: 88.4 us -> 90.7 us
    reshape x10 -> x0, local copies, waits for them, and re-layouts: 13.8 us -> none  [the longest x2 3.65 us: shards(): return (ap.reshape(own, 1, kap, flat), coarse_out.reshape(per, kc, flat))]
    unnamed x4 -> x6, local copies, waits for them, and re-layouts: 1.55 us -> 8.9 us
    reduce_or x3 -> x0, other arithmetic: 2.52 us -> none  [the longest x1 0.91 us: shards(): jnp.any(hit, axis=2)]
    reduce_sum x3 -> x0, other arithmetic: 2.37 us -> none  [the longest x1 0.85 us: shards(): jnp.sum(jnp.where(match, spot[None, :, None, :], 0), axis=3)]
    pallas_call x1, Pallas kernels: 88.4 us -> 90.7 us  [shards(): pl.pallas_call(functools.partial(kernel, (rows, cols, own, ka, kp, kap, k...]
    select_n x4 -> x0, local copies, waits for them, and re-layouts: 1.57 us -> none  [the longest x2 0.81 us: shards(): jnp.where(jnp.any(match, axis=3), jnp.sum(jnp.where(match, spot[None, :,...]
where the time goes in v3:
time: 101 us; the launch traced here: 100 us
  Pallas kernels  90.7 us (90%)
  local copies, waits for them, and re-layouts  8.9 us (9%)
    pallas_call x1, Pallas kernels, shards(): pl.pallas_call(functools.partial(kernel, (rows, cols, own, ka, kp, kap, k...  90.7 us
    unnamed x6, local copies, waits for them, and re-layouts  8.9 us

profile of v3, /device:TPU:0, one launch (start us, length us, event | category | flops | bytes accessed | tf_op | source)
XLA Modules:
  0.0 100.2 jit_solution(6414156060667787360)
XLA Ops:
  0.6 1.3 %copy.9.pcol_ref = s32[8,1,4]{2,1,0:T(1,128)} copy(s32[8,1,4]{0,2,1:T(4,128)} %param.9) | data formatting | bytes 256 | tf_op args[3]
  2.0 1.4 %copy.11.cols_ref = s32[32,8]{1,0:T(8,128)} copy(s32[32,8]{0,1:T(8,128)} %param.11) | data formatting | bytes 2048 | tf_op args[5]
  3.3 1.4 %copy.8.fine_ref = s32[64,1,4]{2,1,0:T(1,128)} copy(s32[64,1,4]{0,2,1:T(4,128)} %param.7) | data formatting | bytes 2048 | tf_op args[1]
  4.7 1.4 %copy.10.kept_ref = s32[64,8]{1,0:T(8,128)} copy(s32[64,8]{0,1:T(8,128)} %param.10) | data formatting | bytes 4096 | tf_op args[4]
  6.1 90.7 %shard_map.77 = (bf16[8,1,8,4096]{3,2,1,0:T(8,128)(2,1)}, f32[1,8,4096]{2,1,0:T(8,128)}) custom-call(bf16[64,1,4,4096]{3,2,1,0:T(4,128)(2,1)} %a_ref.1, bf16[8,1,4,4096]{3,2,1,0:T(4,128)(2,1)} %p_ref.1, s32[64,1,4]{2,1,0:T(1,128)} %copy.8.fine_ref, s32[8,1,4]{2,1,0:T(1,128)} %copy.9.pcol_ref, s32[64,8]{1,0:T(8,128)} %copy.10.kept_ref, s32[32,8]{1,0:T(8,128)} %copy.11.cols_ref), custom_call_target="tpu_custom_call" | custom-call | tf_op jit(solution)/shard_map/pallas_call | solution.py:440
  96.8 1.9 %copy.14 = bf16[8,1,8,4096]{3,2,1,0:T(8,128)(2,1)} copy(bf16[8,1,8,4096]{3,2,1,0:T(8,128)(2,1)} %get-tuple-element.4) | data formatting | bytes 1048576
  98.7 1.6 %copy.15 = f32[1,8,4096]{2,1,0:T(8,128)} copy(f32[1,8,4096]{2,1,0:T(8,128)} %get-tuple-element.5) | data formatting | bytes 262144

commit v4 on v3

--- a/solution.py
+++ b/solution.py
@@ -43,6 +43,10 @@
 
 def unpack(value, scale):
     return value.astype(jnp.int32).astype(F32) * scale
+
+
+def pieces_of(count):
+    return 2 if count % 2 == 0 else 1
 
 
 def gather_tiles(in_left, in_right, picks):
@@ -83,9 +87,9 @@
 
 
 def kernel(
-    sizes, a_ref, p_ref, fine_ref, pcol_ref, kept_ref, cols_ref,
+    sizes, a_ref, p_ref, fine_any, pcol_any, kept_any, cols_any,
     ap_out, coarse_out,
-    a_pre, pg, tables, local, spots, places, local_places, spot_places, rows_in, rows_out,
+    fine_ref, pcol_ref, kept_ref, cols_ref, a_pre, pg, tables, local, spots, places, local_places, spot_places, rows_in, rows_out,
     pl_l, pl_r, pt_l, pt_r, apl, apr,
     s1a, r1a, s2a, r2a, s1a_c, r1a_c, s2a_c, r2a_c, acc_a,
     s1b, r1b, s2b, r2b, s1b_c, r1b_c, s2b_c, r2b_c, acc_b, mine_b, s3, r3, s3_c, r3_c,
@@ -113,6 +117,14 @@
         )
 
     mine = own * kp
+    indices = [
+        pltpu.make_async_copy(src, dst, place_sem.at[3 + n])
+        for n, (src, dst) in enumerate(
+            ((fine_any, fine_ref), (pcol_any, pcol_ref), (kept_any, kept_ref), (cols_any, cols_ref))
+        )
+    ]
+    for copy in indices:
+        copy.start()
 
     def lay_out(u, carry):
         to_rows(p_ref[u, 0].astype(F32), rows_in.at[0], half)
@@ -121,6 +133,52 @@
         return carry
 
     lax.fori_loop(0, own, lay_out, 0)
+    pl.semaphore_wait(barrier, chips + rows - 1)
+
+    def up(h):
+        shard = row - h
+        return (shard >= 0) & (row + 1 < rows), pltpu.make_async_remote_copy(
+            src_ref=pg.at[shard], dst_ref=pg.at[shard],
+            send_sem=up_send.at[h], recv_sem=up_recv.at[h],
+            device_id=(row + 1, col), device_id_type=MESH,
+        )
+
+    def down(h):
+        shard = row + h
+        return (shard < rows) & (row > 0), pltpu.make_async_remote_copy(
+            src_ref=pg.at[shard], dst_ref=pg.at[shard],
+            send_sem=down_send.at[h], recv_sem=down_recv.at[h],
+            device_id=(row - 1, col), device_id_type=MESH,
+        )
+
+    def start(ready, copy):
+        @pl.when(ready)
+        def _():
+            copy.start()
+
+    def done_send(ready, copy):
+        @pl.when(ready)
+        def _():
+            copy.wait_send()
+
+    into = lax.broadcasted_iota(jnp.int32, (width, width), 0)
+    natural = lax.rem(into, 2) * half + into // 2 == lax.broadcasted_iota(jnp.int32, (width, width), 1)
+    natural = natural.astype(F32).astype(BF16)
+
+    def spread(shard):
+        def body(n, carry):
+            pair = jnp.concatenate(halves(pg[shard, n].astype(F32), left), axis=1)
+            pair = jnp.dot(natural, pair, preferred_element_type=F32).astype(BF16)
+            pl_l[shard * mine + n] = pair[:, : 2 * width]
+            pl_r[shard * mine + n] = pair[:, 2 * width :]
+            return carry
+
+        lax.fori_loop(0, mine, body, 0, unroll=4)
+
+    start(*up(0))
+    start(*down(0))
+    for copy in indices:
+        copy.wait()
     lane = lax.broadcasted_iota(jnp.int32, (1, tables.shape[1]), 1)
     lines = []
     for u in range(own):
@@ -138,50 +196,6 @@
     tables[here, :] = jnp.where(lines < mine, lines + row * mine, groups)
     pl_l[groups] = jnp.zeros(pl_l.shape[1:], BF16)
     pl_r[groups] = jnp.zeros(pl_r.shape[1:], BF16)
-    pl.semaphore_wait(barrier, chips + rows - 1)
-
-    def up(h):
-        shard = row - h
-        return (shard >= 0) & (row + 1 < rows), pltpu.make_async_remote_copy(
-            src_ref=pg.at[shard], dst_ref=pg.at[shard],
-            send_sem=up_send.at[h], recv_sem=up_recv.at[h],
-            device_id=(row + 1, col), device_id_type=MESH,
-        )
-
-    def down(h):
-        shard = row + h
-        return (shard < rows) & (row > 0), pltpu.make_async_remote_copy(
-            src_ref=pg.at[shard], dst_ref=pg.at[shard],
-            send_sem=down_send.at[h], recv_sem=down_recv.at[h],
-            device_id=(row - 1, col), device_id_type=MESH,
-        )
-
-    def start(ready, copy):
-        @pl.when(ready)
-        def _():
-            copy.start()
-
-    def done_send(ready, copy):
-        @pl.when(ready)
-        def _():
-            copy.wait_send()
-
-    into = lax.broadcasted_iota(jnp.int32, (width, width), 0)
-    natural = lax.rem(into, 2) * half + into // 2 == lax.broadcasted_iota(jnp.int32, (width, width), 1)
-    natural = natural.astype(F32).astype(BF16)
-
-    def spread(shard):
-        def body(n, carry):
-            pair = jnp.concatenate(halves(pg[shard, n].astype(F32), left), axis=1)
-            pair = jnp.dot(natural, pair, preferred_element_type=F32).astype(BF16)
-            pl_l[shard * mine + n] = pair[:, : 2 * width]
-            pl_r[shard * mine + n] = pair[:, 2 * width :]
-            return carry
-
-        lax.fori_loop(0, mine, body, 0, unroll=4)
-
-    start(*up(0))
-    start(*down(0))
     table_copies = []
     for d in range(1, rows):
         copy = pltpu.make_async_remote_copy(
@@ -258,97 +272,126 @@
         rhs = [gather_tiles(apl, apr, [spot_places[u, c] for c in kept]) for u in range(own)]
         return jnp.dot(lhs, jnp.concatenate(rhs, axis=0), preferred_element_type=F32)
 
+    nx = 2 if chips % 2 == 0 else 1
+    ny = chips // nx
+    chip_y, chip_x = chip // nx, lax.rem(chip, nx)
+
+    def column(step, on):
+        return (lax.rem(chip_y + step[0], ny) * nx + lax.rem(chip_x + step[1], nx)) * 2 + on
+
     def reduce_plane(compute, count, bufs, acc, sems):
         s1, r1, s2, r2, s1_c, r1_c, s2_c, r2_c = bufs
         s1_send, s1_recv, s2_send, s2_recv = sems
-        order = list(range(1, chips)) + [0]
-        first, second = [], []
+        pieces = pieces_of(count)
+        size = count // pieces
+        far = [(dy, 1) for dy in range(1, ny)] if nx == 2 else []
+        along_x = [(0, 1)] if nx == 2 else []
+        along_y = [(dy, 0) for dy in range(1, ny)]
+        plan = []
+        for leg in range(4):
+            for p in range(pieces):
+                x_first = p % 2 == 0
+                if leg == 0:
+                    plan += [(p, d, (0, 1) if x_first else (d[0], 0), []) for d in far]
+                elif leg == 1:
+                    plan += [(p, d, d, []) for d in (along_x if x_first else along_y)]
+                elif leg == 2 and x_first:
+                    plan += [(p, d, d, [(d[0], 1)] if far else []) for d in along_y]
+                elif leg == 2:
+                    plan += [(p, d, d, far) for d in along_x]
+                else:
+                    plan.append((p, (0, 0), None, along_x + along_y))
+        first, second, place = [], [], {}
+
+        def start(src, dst, slot, n, send, recv, device):
+            copies = [
+                pltpu.make_async_remote_copy(
+                    src_ref=a.at[slot], dst_ref=b.at[n], send_sem=send.at[w, n], recv_sem=recv.at[w, n],
+                    device_id=(row, device), device_id_type=MESH,
+                )
+                for w, (a, b) in enumerate(zip(src, dst))
+            ]
+            for copy in copies:
+                copy.start()
+            return copies
 
         def give(n):
-            d = order[n]
-            to = lax.rem(chip + d, chips) * 2 + 1 - core
+            p, d = plan[n][:2]
+            to = column(d, 1 - core)
             slot = n % s1.shape[0]
             if n >= s1.shape[0]:
                 for copy in first[n - s1.shape[0]]:
                     copy.wait_send()
 
             def body(k, carry):
-                s1[slot, k], s1_c[slot, pl.ds(k, 1), :] = pack(compute(to, k))
+                s1[slot, k], s1_c[slot, pl.ds(k, 1), :] = pack(compute(to, p * size + k))
                 return carry
 
-            lax.fori_loop(0, count, body, 0, unroll=2)
-            copies = [
-                pltpu.make_async_remote_copy(
-                    src_ref=src.at[slot], dst_ref=dst.at[n], send_sem=s1_send.at[w, n], recv_sem=s1_recv.at[w, n],
-                    device_id=(row, partner), device_id_type=MESH,
-                )
-                for w, (src, dst) in enumerate(((s1, r1), (s1_c, r1_c)))
-            ]
-            for copy in copies:
-                copy.start()
-            first.append(copies)
+            lax.fori_loop(0, size, body, 0, unroll=2)
+            first.append(start((s1, s1_c), (r1, r1_c), slot, n, s1_send, s1_recv, partner))
+
+        def arrived(p, adds):
+            slots = [place[p, d] for d in adds]
+            for m in slots:
+                for copy in second[m]:
+                    copy.wait_recv()
+            return slots
 
         def finish(n):
-            d = order[n]
-            to = lax.rem(chip + d, chips) * 2 + core
-            slot = n % s2.shape[0]
+            p, d, via, adds = plan[n]
+            to = column(d, core)
+            m = len(second)
+            slot = m % s2.shape[0]
             for copy in first[n]:
                 copy.wait_recv()
-            if d and n >= s2.shape[0]:
-                for copy in second[n - s2.shape[0]]:
+            slots = arrived(p, adds) if via else []
+            if via and m >= s2.shape[0]:
+                for copy in second[m - s2.shape[0]]:
                     copy.wait_send()
 
             def body(k, carry):
-                value = compute(to, k) + unpack(r1[n, k], r1_c[n, pl.ds(k, 1), :])
-                if d:
+                value = compute(to, p * size + k) + unpack(r1[n, k], r1_c[n, pl.ds(k, 1), :])
+                for other in slots:
+                    value = value + unpack(r2[other, k], r2_c[other, pl.ds(k, 1), :])
+                if via:
                     s2[slot, k], s2_c[slot, pl.ds(k, 1), :] = pack(value)
                 else:
-                    acc[k] = value
+                    acc[p * size + k] = value
                 return carry
 
-            lax.fori_loop(0, count, body, 0, unroll=2)
-            if d:
-                copies = [
-                    pltpu.make_async_remote_copy(
-                        src_ref=src.at[slot], dst_ref=dst.at[n], send_sem=s2_send.at[w, n], recv_sem=s2_recv.at[w, n],
-                        device_id=(row, to), device_id_type=MESH,
-                    )
-                    for w, (src, dst) in enumerate(((s2, r2), (s2_c, r2_c)))
-                ]
-                for copy in copies:
-                    copy.start()
-                second.append(copies)
-
-        for n in range(chips):
+            lax.fori_loop(0, size, body, 0, unroll=2)
+            if via:
+                place[p, d] = m
+                second.append(start((s2, s2_c), (r2, r2_c), slot, m, s2_send, s2_recv, column(via, core)))
+
+        for n in range(len(plan)):
             give(n)
             if n:
                 finish(n - 1)
-        finish(chips - 1)
-        for n in range(max(0, chips - s1.shape[0]), chips):
-            for copy in first[n]:
+        finish(len(plan) - 1)
+        for p, _, via, adds in plan:
+            if via is None:
+                slots = arrived(p, adds)
+
+                def body(k, carry):
+                    value = acc[p * size + k]
+                    for other in slots:
+                        value = value + unpack(r2[other, k], r2_c[other, pl.ds(k, 1), :])
+                    acc[p * size + k] = value
+                    return carry
+
+                lax.fori_loop(0, size, body, 0, unroll=2)
+        for copies in first[-s1.shape[0]:] + second[-s2.shape[0]:]:
+            for copy in copies:
                 copy.wait_send()
-        for copies in second:
-            for copy in copies:
-                copy.wait_recv()
-        for n in range(max(0, chips - 1 - s2.shape[0]), chips - 1):
-            for copy in second[n]:
-                copy.wait_send()
-
-        def total(k):
-            value = acc[k]
-            for n in range(chips - 1):
-                value = value + unpack(r2[n, k], r2_c[n, pl.ds(k, 1), :])
-            return value
-
-        return total
-
-    total = reduce_plane(
+
+    reduce_plane(
         product_row, own, (s1a, r1a, s2a, r2a, s1a_c, r1a_c, s2a_c, r2a_c), acc_a,
         (s1a_send, s1a_recv, s2a_send, s2a_recv),
     )
 
     def keep(u, carry):
-        value = total(u).astype(BF16).astype(F32)
+        value = acc_a[u].astype(BF16).astype(F32)
         for s in range(0, kap, 2):
             tile = value[:, s * width : (s + 2) * width]
             x0, x1 = interleave(tile, left)
@@ -366,7 +409,7 @@
     apl[own * kap] = jnp.zeros(apl.shape[1:], BF16)
     apr[own * kap] = jnp.zeros(apr.shape[1:], BF16)
 
-    coarse_total = reduce_plane(
+    reduce_plane(
         coarse_row, rows * per, (s1b, r1b, s2b, r2b, s1b_c, r1b_c, s2b_c, r2b_c), acc_b,
         (s1b_send, s1b_recv, s2b_send, s2b_recv),
     )
@@ -374,7 +417,7 @@
     for d in list(range(1, rows)) + [0]:
         to = lax.rem(row + d, rows)
         for q in range(per):
-            value = coarse_total(to * per + q)
+            value = acc_b[to * per + q]
             if d:
                 s3[d - 1, q], s3_c[d - 1, pl.ds(q, 1), :] = pack(value)
             else:
@@ -420,22 +463,26 @@
     across = -(-coarse // 128) * 128
     chips = cols // 2
     others = max(chips - 1, 1)
-    slots2 = min(others, 3)
     wide = kap * width
     wide_c = kc * width
     vmem = pl.BlockSpec(memory_space=pltpu.VMEM)
-    smem = pl.BlockSpec(memory_space=pltpu.SMEM)
+    anywhere = pl.BlockSpec(memory_space=pl.ANY)
     dma = pltpu.SemaphoreType.DMA
     n_coarse = rows * per
     beyond = max(rows - 1, 1)
 
     def sums(n, across_lanes):
-        depths = (2, chips, slots2, others)
+        pieces = pieces_of(n)
+        depths = (2, chips * pieces, min(others * pieces, 6), others * pieces)
         return [
-            *[pltpu.VMEM((k, n, width, across_lanes), LINK) for k in depths],
-            *[pltpu.VMEM((k, n, across_lanes), F32) for k in depths],
+            *[pltpu.VMEM((k, n // pieces, width, across_lanes), LINK) for k in depths],
+            *[pltpu.VMEM((k, n // pieces, across_lanes), F32) for k in depths],
             pltpu.VMEM((n, width, across_lanes), F32),
         ]
+
+    def signals(n):
+        pieces = pieces_of(n)
+        return [dma((2, k * pieces)) for k in (chips, chips, others, others)]
 
     ap, coarse_out = pl.pallas_call(
         functools.partial(kernel, (rows, cols, own, ka, kp, kap, kc, per, groups)),
@@ -443,9 +490,10 @@
             jax.ShapeDtypeStruct((own, 1, kap, flat), BF16),
             jax.ShapeDtypeStruct((per, kc, flat), F32),
         ),
-        in_specs=[vmem, vmem, smem, smem, smem, smem],
+        in_specs=[vmem, vmem, anywhere, anywhere, anywhere, anywhere],
         out_specs=(vmem, vmem),
         scratch_shapes=[
+            *[pltpu.SMEM(x.shape, jnp.int32) for x in (a_index, p_index, ap_index, coarse_index)],
             pltpu.VMEM((count, width, ka * width), BF16),
             pltpu.VMEM((rows, own * kp, half, lanes), BF16),
             pltpu.VMEM((rows * own, across), jnp.int32),
@@ -469,9 +517,8 @@
             pltpu.VMEM((beyond, per, width, wide_c), LINK),
             pltpu.VMEM((beyond, per, wide_c), F32),
             pltpu.VMEM((beyond, per, wide_c), F32),
-            dma((beyond,)), dma((beyond,)), dma((beyond,)), dma((beyond,)), dma((beyond,)), dma((beyond,)), dma((3,)),
-            dma((2, chips)), dma((2, chips)), dma((2, others)), dma((2, others)),
-            dma((2, chips)), dma((2, chips)), dma((2, others)), dma((2, others)),
+            dma((beyond,)), dma((beyond,)), dma((beyond,)), dma((beyond,)), dma((beyond,)), dma((beyond,)), dma((7,)),
+            *signals(own), *signals(n_coarse),
             dma((2, beyond)), dma((2, beyond)),
         ],
         compiler_params=pltpu.CompilerParams(

time: 101 us -> 87.4 us (0.87)
  Pallas kernels: 90.7 us -> 77.5 us
    pallas_call x1, Pallas kernels: 90.7 us -> 77.5 us  [shards(): pl.pallas_call(functools.partial(kernel, (rows, cols, own, ka, kp, kap, k...]
where the time goes in v4:
time: 87.4 us; the launch traced here: 87 us
  Pallas kernels  77.5 us (89%)
  local copies, waits for them, and re-layouts  8.9 us (10%)
    pallas_call x1, Pallas kernels, shards(): pl.pallas_call(functools.partial(kernel, (rows, cols, own, ka, kp, kap, k...  77.5 us
    unnamed x6, local copies, waits for them, and re-layouts  8.9 us

profile of v4, /device:TPU:0, one launch (start us, length us, event | category | flops | bytes accessed | tf_op | source)
XLA Modules:
  0.0 87.0 jit_solution(16532990384641647298)
XLA Ops:
  0.6 1.3 %copy.9.pcol_any = s32[8,1,4]{2,1,0:T(1,128)} copy(s32[8,1,4]{0,2,1:T(4,128)} %param.9) | data formatting | bytes 256 | tf_op args[3]
  2.0 1.4 %copy.11.cols_any = s32[32,8]{1,0:T(8,128)} copy(s32[32,8]{0,1:T(8,128)} %param.11) | data formatting | bytes 2048 | tf_op args[5]
  3.3 1.4 %copy.8.fine_any = s32[64,1,4]{2,1,0:T(1,128)} copy(s32[64,1,4]{0,2,1:T(4,128)} %param.7) | data formatting | bytes 2048 | tf_op args[1]
  4.7 1.4 %copy.10.kept_any = s32[64,8]{1,0:T(8,128)} copy(s32[64,8]{0,1:T(8,128)} %param.10) | data formatting | bytes 4096 | tf_op args[4]
  6.1 77.5 %shard_map.77 = (bf16[8,1,8,4096]{3,2,1,0:T(8,128)(2,1)}, f32[1,8,4096]{2,1,0:T(8,128)}) custom-call(bf16[64,1,4,4096]{3,2,1,0:T(4,128)(2,1)} %a_ref.1, bf16[8,1,4,4096]{3,2,1,0:T(4,128)(2,1)} %p_ref.1, s32[64,1,4]{2,1,0:T(1,128)} %copy.8.fine_any, s32[8,1,4]{2,1,0:T(1,128)} %copy.9.pcol_any, s32[64,8]{1,0:T(8,128)} %copy.10.kept_any, s32[32,8]{1,0:T(8,128)} %copy.11.cols_any), custom_call_target="tpu_custom_call" | custom-call | tf_op jit(solution)/shard_map/pallas_call | solution.py:487
  83.6 1.9 %copy.14 = bf16[8,1,8,4096]{3,2,1,0:T(8,128)(2,1)} copy(bf16[8,1,8,4096]{3,2,1,0:T(8,128)(2,1)} %get-tuple-element.4) | data formatting | bytes 1048576
  85.4 1.6 %copy.15 = f32[1,8,4096]{2,1,0:T(8,128)} copy(f32[1,8,4096]{2,1,0:T(8,128)} %get-tuple-element.5) | data formatting | bytes 262144

commit v5 on v4

--- a/solution.py
+++ b/solution.py
@@ -184,11 +184,11 @@
     for u in range(own):
         line = jnp.full(lane.shape, mine, jnp.int32)
         for m in range(kp):
-            line = jnp.where(lane == pcol_ref[u, 0, m], u * kp + m, line)
+            line = jnp.where(lane == pcol_ref[0, m, u], u * kp + m, line)
         lines.append(line)
         spot = jnp.full(lane.shape, own * kap, jnp.int32)
         for n in range(kap):
-            spot = jnp.where(lane == kept_ref[u * cols + col, n], u * kap + n, spot)
+            spot = jnp.where(lane == kept_ref[n, u * cols + col], u * kap + n, spot)
         spots[u : u + 1, :] = spot
     lines = jnp.concatenate(lines, axis=0)
     local[...] = lines
@@ -260,15 +260,15 @@
 
     def product_row(to, u):
         i = u * cols + to
-        kept = [kept_ref[i, n] for n in range(kap)]
-        fine = [fine_ref[i, 0, e] for e in range(ka)]
+        kept = [kept_ref[n, i] for n in range(kap)]
+        fine = [fine_ref[0, e, i] for e in range(ka)]
         rhs = [gather_tiles(pl_l, pl_r, [places[k, j] for j in kept]) for k in fine]
         return jnp.dot(a_pre[i], jnp.concatenate(rhs, axis=0), preferred_element_type=F32)
 
     def coarse_row(to, n):
         j = ((n // per) * cols + to) * per + lax.rem(n, per)
         lhs = gather_tiles(pt_l, pt_r, [local_places[u, j] for u in range(own)])
-        kept = [cols_ref[j, t] for t in range(kc)]
+        kept = [cols_ref[t, j] for t in range(kc)]
         rhs = [gather_tiles(apl, apr, [spot_places[u, c] for c in kept]) for u in range(own)]
         return jnp.dot(lhs, jnp.concatenate(rhs, axis=0), preferred_element_type=F32)
 
@@ -459,6 +459,7 @@
     half = width // 2
     lanes = 2 * width
 
+    turned = (a_index.transpose(1, 2, 0), p_index.transpose(1, 2, 0), ap_index.T, coarse_index.T)
     groups = rows * own * kp
     across = -(-coarse // 128) * 128
     chips = cols // 2
@@ -493,7 +494,7 @@
         in_specs=[vmem, vmem, anywhere, anywhere, anywhere, anywhere],
         out_specs=(vmem, vmem),
         scratch_shapes=[
-            *[pltpu.SMEM(x.shape, jnp.int32) for x in (a_index, p_index, ap_index, coarse_index)],
+            *[pltpu.SMEM(x.shape, jnp.int32) for x in turned],
             pltpu.VMEM((count, width, ka * width), BF16),
             pltpu.VMEM((rows, own * kp, half, lanes), BF16),
             pltpu.VMEM((rows * own, across), jnp.int32),
@@ -524,7 +525,7 @@
         compiler_params=pltpu.CompilerParams(
             collective_id=0, has_side_effects=True, vmem_limit_bytes=60 * 1024 * 1024
         ),
-    )(a_blocks, p_blocks, a_index, p_index, ap_index, coarse_index)
+    )(a_blocks, p_blocks, *turned)
     return ap, coarse_out
 
 

time: 87.4 us -> 81.9 us (0.937)
  local copies, waits for them, and re-layouts: 8.9 us -> 3.44 us
    unnamed x6 -> x2, local copies, waits for them, and re-layouts: 8.9 us -> 3.44 us
where the time goes in v5:
time: 81.9 us; the launch traced here: 81.6 us
  Pallas kernels  77.6 us (95%)
  local copies, waits for them, and re-layouts  3.44 us (4%)
    pallas_call x1, Pallas kernels, shards(): pl.pallas_call(functools.partial(kernel, (rows, cols, own, ka, kp, kap, k...  77.6 us
    unnamed x2, local copies, waits for them, and re-layouts  3.44 us

profile of v5, /device:TPU:0, one launch (start us, length us, event | category | flops | bytes accessed | tf_op | source)
XLA Modules:
  0.0 81.6 jit_solution(17416850703021452541)
XLA Ops:
  0.6 77.6 %shard_map.77 = (bf16[8,1,8,4096]{3,2,1,0:T(8,128)(2,1)}, f32[1,8,4096]{2,1,0:T(8,128)}) custom-call(bf16[64,1,4,4096]{3,2,1,0:T(4,128)(2,1)} %a_ref.1, bf16[8,1,4,4096]{3,2,1,0:T(4,128)(2,1)} %p_ref.1, s32[1,4,64]{2,1,0:T(4,128)} %bitcast.6, s32[1,4,8]{2,1,0:T(4,128)} %bitcast.7, s32[8,64]{1,0:T(8,128)} %bitcast.4, s32[8,32]{1,0:T(8,128)} %bitcast.5), custom_call_target="tpu_custom_call" | custom-call | tf_op jit(solution)/shard_map/pallas_call | solution.py:488
  78.2 1.9 %copy.10 = bf16[8,1,8,4096]{3,2,1,0:T(8,128)(2,1)} copy(bf16[8,1,8,4096]{3,2,1,0:T(8,128)(2,1)} %get-tuple-element.4) | data formatting | bytes 1048576
  80.1 1.6 %copy.11 = f32[1,8,4096]{2,1,0:T(8,128)} copy(f32[1,8,4096]{2,1,0:T(8,128)} %get-tuple-element.5) | data formatting | bytes 262144
